TPU v7x, 32 devices: a whole 2x2x4 slice. The times are simulated.
32 devices in a mesh: fsdp: 4 (over z), rep: 8 (over y, x, core).
Axes of the slice: x: 2, y: 2, z: 4, core: 2. Of those that a mesh axis runs over, the one named last changes fastest.
Arguments:
- tokens: bfloat16 [8, 2048, 768], P('rep', 'fsdp'), may hold values from -6 to 6
- attention_gain: bfloat16 [768], P('fsdp'), may hold values from 0.25 to 1.75
- projection_in: bfloat16 [768, 2304], P('fsdp'), may hold values from -0.21875 to 0.21875
- attention_out: bfloat16 [768, 768], P('fsdp'), may hold values from -6 to 6
- feedforward_gain: bfloat16 [768], P('fsdp'), may hold values from 0.25 to 1.75
- expansion: bfloat16 [768, 2304], P('fsdp'), may hold values from -0.21875 to 0.21875
- contraction: bfloat16 [1152, 768], P('fsdp'), may hold values from -0.1875 to 0.1875
- cotangent: bfloat16 [8, 2048, 768], P('rep', 'fsdp'), may hold values from -6 to 6
Outputs:
- block_output: bfloat16 [8, 2048, 768], P('rep', 'fsdp')
- token_grad: float32 [8, 2048, 768], P('rep', 'fsdp')
- attention_gain_grad: float32 [768], P('fsdp')
- projection_in_grad: float32 [768, 2304], P('fsdp')
- attention_out_grad: float32 [768, 768], P('fsdp')
- feedforward_gain_grad: float32 [768], P('fsdp')
- expansion_grad: float32 [768, 2304], P('fsdp')
- contraction_grad: float32 [1152, 768], P('fsdp')
All inputs are finite; a program needn't handle non-finite values.
Results may differ from a plain program's by a relative error of at most 0.018.
Values may be sent and summed in bfloat16 or wider, within the bound.
No kernel may reach another device: no remote copies, remote signals or barrier semaphores. Data moves between devices by JAX's collectives and lax.ppermute only.
A program may use at most 128 MiB of HBM per device.

v0:
```python
import functools
import math

import jax
import jax.numpy as jnp
from jax import lax
from jax.experimental import pallas as pl
from jax.experimental.pallas import tpu as pltpu
from jax.sharding import PartitionSpec as P

HEADS = 12
HEAD_DIM = 64
HALF = HEAD_DIM // 2
SCALE = 1.0 / math.sqrt(HEAD_DIM)
EPS = 1e-05
THETA = 160000.0
F32 = jnp.float32
BF16 = jnp.bfloat16
NN = (((1,), (0,)), ((), ()))
NT = (((1,), (1,)), ((), ()))
TN = (((0,), (0,)), ((), ()))
TT = (((0,), (1,)), ((), ()))


def mul(a, b, dims=NN):
    return lax.dot_general(a, b, dims, preferred_element_type=F32)


def attend_kernel(q_ref, k_ref, v_ref, out_ref, log_ref):
    scores = mul(k_ref[...].T, q_ref[...])
    highest = jnp.max(scores, axis=0, keepdims=True)
    raised = jnp.exp(scores - highest)
    total = jnp.sum(raised, axis=0, keepdims=True)
    mixed = mul(v_ref[...], raised.astype(BF16))
    out_ref[...] = (mixed / total).astype(BF16)
    log_ref[...] = highest + jnp.log(total)


def attend(head, queries, keys, values, step=1024):
    count = queries.shape[1]
    step = min(step, count)
    whole = pl.BlockSpec((HEAD_DIM, count), lambda i: (head, 0))
    return pl.pallas_call(
        attend_kernel,
        grid=(count // step,),
        in_specs=[pl.BlockSpec((HEAD_DIM, step), lambda i: (head, i)), whole, whole],
        out_specs=[
            pl.BlockSpec((HEAD_DIM, step), lambda i: (0, i)),
            pl.BlockSpec((1, step), lambda i: (0, i)),
        ],
        out_shape=[
            jax.ShapeDtypeStruct((HEAD_DIM, count), BF16),
            jax.ShapeDtypeStruct((1, count), F32),
        ],
        compiler_params=pltpu.CompilerParams(vmem_limit_bytes=26 * 2**20),
        cost_estimate=pl.CostEstimate(
            flops=28 * count * count * HEAD_DIM,
            bytes_accessed=8 * HEAD_DIM * count,
            transcendentals=count * count,
        ),
        name="attend",
    )(queries, keys, values)


def turn_back(values, cosine, sine):
    first, second = values[:HALF], values[HALF:]
    return jnp.concatenate([first * cosine + second * sine, second * cosine - first * sine], axis=0)


def attend_back_kernel(
    q_ref, kt_ref, vt_ref, u0_ref, u1_ref, u2_ref, u3_ref, out_ref, log_ref, cos_ref, sin_ref, normed_ref,
    grad_ref, weight_ref, up_ref, k_ref, v_ref, dk_ref, dv_ref,
):
    index = pl.program_id(0)
    step = q_ref.shape[1]

    @pl.when(index == 0)
    def _():
        for d, ref in enumerate((u0_ref, u1_ref, u2_ref, u3_ref)):
            up_ref[d] = ref[...]
        k_ref[...] = kt_ref[...].T
        v_ref[...] = vt_ref[...].T
        dk_ref[...] = jnp.zeros_like(dk_ref)
        dv_ref[...] = jnp.zeros_like(dv_ref)

    upstream = up_ref[index]
    inner_sum = jnp.sum(upstream.astype(F32) * out_ref[...].astype(F32), axis=0, keepdims=True)
    chances = jnp.exp(mul(k_ref[...], q_ref[...]) - log_ref[...])
    prob_back = mul(v_ref[...], upstream)
    score_back = (chances * (prob_back - inner_sum)).astype(BF16)
    dv_ref[...] += mul(chances.astype(BF16), upstream, NT)
    dk_ref[...] += mul(score_back, q_ref[...], NT)
    columns = pl.ds(pl.multiple_of(index * step, step), step)
    query_back = mul(kt_ref[...], score_back) * SCALE
    grad_ref[pl.ds(0, HEAD_DIM), columns] = turn_back(
        query_back, cos_ref[:, columns], sin_ref[:, columns]
    ).astype(BF16)

    @pl.when(index == pl.num_programs(0) - 1)
    def _():
        key_back = turn_back(dk_ref[...].T, cos_ref[...], sin_ref[...])
        grad_ref[pl.ds(HEAD_DIM, HEAD_DIM), :] = key_back.astype(BF16)
        grad_ref[pl.ds(2 * HEAD_DIM, HEAD_DIM), :] = dv_ref[...].T.astype(BF16)
        weight_ref[...] = mul(grad_ref[...], normed_ref[...]).astype(BF16)


def attend_back(head, queries, keys, values, upstream, merged, log, cosine, sine, normed):
    count, width = normed.shape
    step = upstream[0].shape[1]
    some = pl.BlockSpec((HEAD_DIM, step), lambda i: (head, i))
    whole = pl.BlockSpec((HEAD_DIM, count), lambda i: (head, 0))
    table = pl.BlockSpec((HALF, count), lambda i: (0, 0))
    return pl.pallas_call(
        attend_back_kernel,
        grid=(count // step,),
        in_specs=[
            some,
            whole,
            whole,
            *[pl.BlockSpec((HEAD_DIM, step), lambda i: (head, 0))] * len(upstream),
            some,
            pl.BlockSpec((1, step), lambda i: (0, i)),
            table,
            table,
            pl.BlockSpec((count, width), lambda i: (0, 0)),
        ],
        out_specs=[
            pl.BlockSpec((3 * HEAD_DIM, count), lambda i: (0, 0)),
            pl.BlockSpec((3 * HEAD_DIM, width), lambda i: (0, 0)),
        ],
        out_shape=[
            jax.ShapeDtypeStruct((3 * HEAD_DIM, count), BF16),
            jax.ShapeDtypeStruct((3 * HEAD_DIM, width), BF16),
        ],
        scratch_shapes=[
            pltpu.VMEM((len(upstream), HEAD_DIM, step), BF16),
            pltpu.VMEM((count, HEAD_DIM), BF16),
            pltpu.VMEM((count, HEAD_DIM), BF16),
            pltpu.VMEM((count, HEAD_DIM), F32),
            pltpu.VMEM((count, HEAD_DIM), F32),
        ],
        compiler_params=pltpu.CompilerParams(vmem_limit_bytes=24 * 2**20),
        cost_estimate=pl.CostEstimate(
            flops=56 * count * count * HEAD_DIM,
            bytes_accessed=16 * HEAD_DIM * count,
            transcendentals=count * count,
        ),
        name="attend_back",
    )(queries, keys, values, *upstream, merged, log, cosine, sine, normed)


def row_copies(place_ref, mine, other, buffer, sems):
    z, core = place_ref[0], place_ref[1]
    size, rows, _ = mine.shape
    copies = []
    for d in range(size):
        for k, (ref, side) in enumerate(((mine, core), (other, 1 - core))):
            target = buffer.at[z ^ d, pl.ds(pl.multiple_of(side * rows, 16), rows), :]
            copies.append(pltpu.make_async_copy(ref.at[d], target, sems.at[d, k]))
    return copies


def unit_of(values):
    centre = values - jnp.mean(values, axis=-1, keepdims=True)
    inverse = lax.rsqrt(jnp.mean(centre * centre, axis=-1, keepdims=True) + EPS)
    return centre * inverse, inverse


def turn(values, cosine, sine):
    first, second = values[:HALF], values[HALF:]
    return jnp.concatenate([first * cosine - second * sine, second * cosine + first * sine], axis=0)


def project_kernel(
    place_ref, pair_ref, other_ref, gain_ref, cos_ref, sin_ref, mine_ref, theirs_ref,
    normed_ref, q_ref, kt_ref, vt_ref, buffer, weight, sems,
):
    index = pl.program_id(0)
    part = q_ref.shape[0]
    size = buffer.shape[0]

    @pl.when(index == 0)
    def _():
        for copy in row_copies(place_ref, mine_ref, theirs_ref, buffer, sems):
            copy.start()

    block = jnp.where(index < 2, pair_ref[...].astype(F32), other_ref[...].astype(F32))
    normed = (unit_of(block)[0] * gain_ref[...]).astype(BF16)
    normed_ref[...] = normed

    @pl.when(index == 0)
    def _():
        for copy in row_copies(place_ref, mine_ref, theirs_ref, buffer, sems):
            copy.wait()
        start = pl.multiple_of(place_ref[1] * 2 * part, 128)
        odd = place_ref[0] & 1 == 1
        for t in range(3):
            both = buffer[:, t * part : (t + 1) * part, pl.ds(start, 2 * part)].reshape(size * part, 2 * part)
            chosen = jnp.where(odd, both[:, part:].astype(F32), both[:, :part].astype(F32))
            weight[:, t * part : (t + 1) * part] = chosen.astype(BF16)

    projected = mul(normed, weight[...])
    turned = projected[:, : 2 * part].T
    cosine, sine = cos_ref[...], sin_ref[...]
    for head in range(part // HEAD_DIM):
        rows = slice(head * HEAD_DIM, (head + 1) * HEAD_DIM)
        queries = turn(turned[rows], cosine, sine).astype(BF16)
        q_ref[rows, :] = (queries.astype(F32) * SCALE).astype(BF16)
        keys = turn(turned[part + head * HEAD_DIM : part + (head + 1) * HEAD_DIM], cosine, sine)
        kt_ref[rows, :] = keys.astype(BF16)
    vt_ref[...] = projected[:, 2 * part :].astype(BF16).T


def project(where, pair, other, gain, cosine, sine, mine, theirs, count):
    width = pair.shape[1]
    size, rows = mine.shape[0], 2 * mine.shape[1]
    part = width // size
    total = size * count
    anywhere = pl.BlockSpec(memory_space=pl.ANY)
    columns = pl.BlockSpec((part, count), lambda i: (0, i))
    return pl.pallas_call(
        project_kernel,
        grid=(size,),
        in_specs=[
            pl.BlockSpec(memory_space=pltpu.SMEM),
            pl.BlockSpec((count, width), lambda i: (jnp.minimum(i, 1), 0)),
            pl.BlockSpec((count, width), lambda i: (jnp.maximum(i - 2, 0), 0)),
            pl.BlockSpec((1, width), lambda i: (0, 0)),
            pl.BlockSpec((HALF, count), lambda i: (0, i)),
            pl.BlockSpec((HALF, count), lambda i: (0, i)),
            anywhere,
            anywhere,
        ],
        out_specs=[
            pl.BlockSpec((count, width), lambda i: (i, 0)),
            columns,
            columns,
            columns,
        ],
        out_shape=[
            jax.ShapeDtypeStruct((total, width), BF16),
            jax.ShapeDtypeStruct((part, total), BF16),
            jax.ShapeDtypeStruct((part, total), BF16),
            jax.ShapeDtypeStruct((part, total), BF16),
        ],
        scratch_shapes=[
            pltpu.VMEM((size, rows, width), BF16),
            pltpu.VMEM((width, 3 * part), BF16),
            pltpu.SemaphoreType.DMA((size, 2)),
        ],
        compiler_params=pltpu.CompilerParams(vmem_limit_bytes=18 * 2**20),
        cost_estimate=pl.CostEstimate(flops=8 * 10**9, bytes_accessed=20 * 10**6, transcendentals=0),
        name="project",
    )(where, pair, other, gain, cosine, sine, mine, theirs)


def forward_back_kernel(
    place_ref, m0_ref, m1_ref, m2_ref, m3_ref, tokens_ref, up_ref, gain_ref, mine_ref, theirs_ref,
    result_ref, state_back_ref, low_ref, normed_ref, active_ref, inner_back_ref, b0_ref, b1_ref, b2_ref, b3_ref,
    buffer, sems,
):
    part, width = m0_ref.shape[0], tokens_ref.shape[1]
    size = buffer.shape[0]
    hidden = active_ref.shape[1]
    z = place_ref[0]

    @pl.when(pl.program_id(0) == 0)
    def _():
        copies = row_copies(place_ref, mine_ref, theirs_ref, buffer, sems)
        for copy in copies:
            copy.start()
        for copy in copies:
            copy.wait()

    expand = [buffer[:, (1 + t) * part : (2 + t) * part, :].reshape(width, width) for t in range(3)]
    contract = buffer[:, 4 * part : 4 * part + hidden // size, :].reshape(hidden, width)
    gain = gain_ref[...]

    state = tokens_ref[...].astype(F32)
    for k, ref in enumerate((m0_ref, m1_ref, m2_ref, m3_ref)):
        state = state + mul(ref[...], buffer[z ^ k, :part, :], TN)
    unit, inverse = unit_of(state)
    normed = (unit * gain).astype(BF16)
    normed_ref[...] = normed
    inner = jnp.concatenate([mul(normed, weight) for weight in expand], axis=1)
    first, second = inner[:, :hidden], inner[:, hidden:]
    chance = 0.5 + 0.5 * lax.erf(first * math.sqrt(0.5))
    gated = first * chance
    slope = chance + first * (jnp.exp(-0.5 * first * first) * (1.0 / math.sqrt(2.0 * math.pi)))
    active = (gated * second).astype(BF16)
    active_ref[...] = active
    result_ref[...] = (state + mul(active, contract)).astype(BF16)

    upstream = up_ref[...]
    active_back = mul(upstream, contract, NT).astype(BF16).astype(F32)
    inner_back = jnp.concatenate(
        [(active_back * second * slope).astype(BF16), (active_back * gated).astype(BF16)], axis=1
    )
    inner_back_ref[...] = inner_back
    normed_back = mul(inner_back[:, :width], expand[0], NT)
    normed_back = normed_back + mul(inner_back[:, width : 2 * width], expand[1], NT)
    normed_back = normed_back + mul(inner_back[:, 2 * width :], expand[2], NT)
    scaled = normed_back * gain
    mean = jnp.mean(scaled, axis=-1, keepdims=True)
    lean = jnp.mean(scaled * unit, axis=-1, keepdims=True)
    state_back = upstream.astype(F32) + inverse * (scaled - mean - unit * lean)
    state_back_ref[...] = state_back
    low = state_back.astype(BF16)
    low_ref[...] = low
    for k, ref in enumerate((b0_ref, b1_ref, b2_ref, b3_ref)):
        ref[...] = mul(buffer[z ^ k, :part, :], low, NT).astype(BF16)


def forward_back(where, merged, tokens, upstream, gain, sides, hidden, step=256):
    count, width = tokens.shape
    size, rows = sides[0].shape[0], 2 * sides[0].shape[1]
    part = width // size
    anywhere = pl.BlockSpec(memory_space=pl.ANY)
    columns = pl.BlockSpec((part, step), lambda i: (0, i))

    def some(lanes):
        return pl.BlockSpec((step, lanes), lambda i: (i, 0))

    lanes = [width, width, width, width, hidden, 2 * hidden]
    kinds = [BF16, F32, BF16, BF16, BF16, BF16]
    return pl.pallas_call(
        forward_back_kernel,
        grid=(count // step,),
        in_specs=[pl.BlockSpec(memory_space=pltpu.SMEM)]
        + [columns] * size
        + [some(width), some(width), pl.BlockSpec((1, width), lambda i: (0, 0))]
        + [anywhere] * len(sides),
        out_specs=[some(n) for n in lanes] + [columns] * size,
        out_shape=[jax.ShapeDtypeStruct((count, n), kind) for n, kind in zip(lanes, kinds)]
        + [jax.ShapeDtypeStruct((part, count), BF16)] * size,
        scratch_shapes=[pltpu.VMEM((size, rows, width), BF16), pltpu.SemaphoreType.DMA((size, 2))],
        compiler_params=pltpu.CompilerParams(vmem_limit_bytes=26 * 2**20),
        cost_estimate=pl.CostEstimate(flops=14 * 10**9, bytes_accessed=20 * 10**6, transcendentals=0),
        name="forward_back",
    )(where, *merged, tokens, upstream, gain, *sides)


def gradients_kernel(
    place_ref, m0_ref, m1_ref, m2_ref, m3_ref, up_ref, low_ref, normed_ref, active_ref, inner_back_ref,
    kept_ref, sent_ref,
):
    z, core = place_ref[0], place_ref[1]
    part, width = m0_ref.shape[0], up_ref.shape[1]
    size, rows, lanes = kept_ref.shape
    held = active_ref.shape[1] // size
    for grads_ref, side in ((sent_ref, 1 - core), (kept_ref, core)):
        start = pl.multiple_of(side * lanes, 128)
        low = low_ref[:, pl.ds(start, lanes)]
        for k, ref in enumerate((m0_ref, m1_ref, m2_ref, m3_ref)):
            grads_ref[z ^ k, :part, :] = mul(ref[...], low).astype(BF16)
        normed = normed_ref[...]
        for t in range(3):
            grad = mul(normed, inner_back_ref[:, pl.ds(t * width + start, lanes)], TN)
            grads_ref[:, (1 + t) * part : (2 + t) * part, :] = grad.astype(BF16).reshape(size, part, lanes)
        grad = mul(active_ref[...], up_ref[:, pl.ds(start, lanes)], TN)
        grads_ref[:, 4 * part : 4 * part + held, :] = grad.astype(BF16).reshape(size, held, lanes)
        if rows > 4 * part + held:
            grads_ref[:, 4 * part + held :, :] = jnp.zeros((size, rows - 4 * part - held, lanes), BF16)


def gradients(where, merged, upstream, low, normed, active, inner_back, rows):
    size = len(merged)
    inside = pl.BlockSpec(memory_space=pltpu.VMEM)
    return pl.pallas_call(
        gradients_kernel,
        in_specs=[pl.BlockSpec(memory_space=pltpu.SMEM)] + [inside] * (size + 5),
        out_specs=[inside] * 2,
        out_shape=[jax.ShapeDtypeStruct((size, rows, upstream.shape[1] // 2), BF16)] * 2,
        compiler_params=pltpu.CompilerParams(vmem_limit_bytes=22 * 2**20),
        cost_estimate=pl.CostEstimate(flops=12 * 10**9, bytes_accessed=12 * 10**6, transcendentals=0),
        name="gradients",
    )(where, *merged, upstream, low, normed, active, inner_back)


def token_kernel(heads, place_ref, *refs):
    size = len(refs[: -9]) // heads
    pieces = refs[: heads * size]
    mine_ref, theirs_ref, tokens_ref, back_ref, gain_ref, grad_ref, parts, buffer, sems = refs[heads * size :]
    z = place_ref[0]
    width = buffer.shape[2]
    part = width // size
    copies = row_copies(place_ref, mine_ref, theirs_ref, buffer, sems)
    for copy in copies:
        copy.start()
    for head in range(heads):
        for k in range(size):
            ref = pieces[head * size + k]
            lines = pl.ds(pl.multiple_of((z ^ k) * part + head * HEAD_DIM, HEAD_DIM), HEAD_DIM)
            for t in range(3):
                parts[t, lines, :] = ref[t * HEAD_DIM : (t + 1) * HEAD_DIM, :]
    for copy in copies:
        copy.wait()
    total = jnp.zeros((width, tokens_ref.shape[0]), F32)
    for t in range(3):
        total = total + mul(buffer[:, t * part : (t + 1) * part, :].reshape(width, width), parts[t])
    unit, inverse = unit_of(tokens_ref[...].astype(F32))
    scaled = total.T * gain_ref[...]
    mean = jnp.mean(scaled, axis=-1, keepdims=True)
    lean = jnp.mean(scaled * unit, axis=-1, keepdims=True)
    grad_ref[...] = back_ref[...] + inverse * (scaled - mean - unit * lean)


def token_back(where, received, mine, theirs, tokens, state_back, gain):
    count, width = tokens.shape
    size, rows = mine.shape[0], 2 * mine.shape[1]
    inside = pl.BlockSpec(memory_space=pltpu.VMEM)
    anywhere = pl.BlockSpec(memory_space=pl.ANY)
    pieces = [piece for rounds in received for piece in rounds]
    return pl.pallas_call(
        functools.partial(token_kernel, len(received)),
        in_specs=[pl.BlockSpec(memory_space=pltpu.SMEM)]
        + [inside] * len(pieces)
        + [anywhere] * 2
        + [inside] * 3,
        out_specs=inside,
        out_shape=jax.ShapeDtypeStruct((count, width), F32),
        scratch_shapes=[
            pltpu.VMEM((3, width, count), BF16),
            pltpu.VMEM((size, rows, width), BF16),
            pltpu.SemaphoreType.DMA((size, 2)),
        ],
        compiler_params=pltpu.CompilerParams(vmem_limit_bytes=18 * 2**20),
        cost_estimate=pl.CostEstimate(flops=5 * 10**9, bytes_accessed=12 * 10**6, transcendentals=0),
        name="token_back",
    )(where, *pieces, mine, theirs, tokens, state_back, gain)


def after(values, *others):
    return lax.optimization_barrier((values, others))[0]


def swap(values, axis, size, offset):
    return lax.ppermute(values, axis, [(i, i ^ offset) for i in range(size)])


def exchange(pieces, size):
    return [pieces[0]] + [swap(pieces[d], "fsdp", size, d) for d in range(1, size)]


def column(values, size, ranks, pairs):
    full = [
        (z * ranks + r, to * ranks + (r & ~1) + core)
        for z in range(size)
        for r in range(ranks)
        for to, core in pairs(z, r & 1)
    ]
    return lax.ppermute(values, ("fsdp", "rep"), full)


def collect(own, home, size, ranks, early):
    first = column(
        own, size, ranks, lambda z, c: [(z ^ 1, c) if c == z >> 1 else (z ^ 2, 1 - c)]
    )
    second = column(first, size, ranks, lambda z, c: [] if c == z >> 1 else [(z ^ 1, c)])
    low = jnp.where(home, own, first)
    high = jnp.where(home, first, second)
    pair, early = after((jnp.concatenate([low, high], axis=0), early))
    other = swap(pair, "rep", ranks, 1)
    return pair, other, first, second, early


def trade_out(pieces, size, ranks, rounds=None):
    def round_of(k):
        return lambda z, c: [((2 * c + (z & 1)) ^ k, z >> 1)]

    return [column(pieces[k], size, ranks, round_of(k)) for k in rounds or range(size)]


def trade_back(pieces, size, ranks):
    def round_of(k):
        return lambda z, c: [(2 * c + ((z ^ k) & 1), (z ^ k) >> 1)]

    return [column(pieces[k], size, ranks, round_of(k)) for k in range(size)]


def pick(blocks, index):
    return lax.dynamic_index_in_dim(blocks, index, 0, keepdims=False)


def reorder(blocks, z, size):
    return jnp.stack([pick(blocks, z ^ j) for j in range(size)])


def far(ranks):
    bits = []
    bit = 2
    while bit < ranks:
        bits.append(bit)
        bit *= 2
    return bits


def stage_bit(core, ranks, stage):
    bits = far(ranks)
    return bits[stage] if core == 0 else bits[len(bits) - 1 - stage]


def stage_swap(values, ranks, stage):
    return lax.ppermute(values, "rep", [(i, i ^ stage_bit(i & 1, ranks, stage)) for i in range(ranks)])


def stage_upper(r, ranks, stage):
    bit = jnp.where(r & 1 == 0, stage_bit(0, ranks, stage), stage_bit(1, ranks, stage))
    return r & bit != 0


def place(r, ranks):
    stages = len(far(ranks))
    total = jnp.where(r & 1 != 0, 1 << stages, 0)
    for stage in range(stages):
        total = total + jnp.where(stage_upper(r, ranks, stage), 1 << stage, 0)
    return total


def join(mine, other, upper):
    return jnp.concatenate([jnp.where(upper, other, mine), jnp.where(upper, mine, other)], axis=1)


def cut(values, upper):
    half = values.shape[1] // 2
    mine = jnp.where(upper, half, 0)
    sent = lax.dynamic_slice_in_dim(values, half - mine, half, 1)
    return sent, lax.dynamic_slice_in_dim(values, mine, half, 1)


def add(one, two):
    return (one.astype(F32) + two.astype(F32)).astype(BF16)


def grow(values, r, ranks, stages):
    for stage in stages:
        values = join(values, stage_swap(values, ranks, stage), stage_upper(r, ranks, stage))
    return values


def grow_flat(values, r, ranks, stages):
    for stage in stages:
        other = stage_swap(values, ranks, stage)
        upper = stage_upper(r, ranks, stage)
        values = jnp.concatenate(
            [jnp.where(upper, other, values), jnp.where(upper, values, other)], axis=0
        )
    return values


def shrink(values, r, ranks, stages):
    for stage in stages:
        sent, kept = cut(values, stage_upper(r, ranks, stage))
        values = add(kept, stage_swap(sent, ranks, stage))
    return values


def halves(values):
    middle = values.shape[-1] // 2
    return [values[..., :middle], values[..., middle:]]


def split_rows(shard, r, ranks):
    rows = shard.shape[0] // ranks
    return lax.dynamic_slice_in_dim(shard, place(r, ranks) * rows, rows, 0)


def finish_kernel(
    place_ref, mine_ref, other_ref, into_ref, expand_ref, gain_a_ref, gain_b_ref,
    into_sum_ref, gain_a_sum_ref, out_sum_ref, expand_sum_ref, gain_b_sum_ref, contract_sum_ref,
):
    first = place_ref[1] == 0
    part, width = out_sum_ref.shape
    held = contract_sum_ref.shape[0]
    pieces = mine_ref.shape[0]
    lines = 3 * part // pieces

    def gathered(start):
        rows = mine_ref.shape[1] if start else lines
        sides = []
        for one, two in ((mine_ref, other_ref), (other_ref, mine_ref)):
            blocks = [
                jnp.where(first, one[p, start:rows].astype(F32), two[p, start:rows].astype(F32))
                for p in range(pieces)
            ]
            sides.append(jnp.concatenate(blocks, axis=0))
        return sides

    blocks = [side[:, k * part : (k + 1) * part].T for side in gathered(0) for k in range(2)]
    total = jnp.zeros((part, 1), F32)
    for t in range(3):
        row = jnp.concatenate([block[:, t * part : (t + 1) * part] for block in blocks], axis=1)
        into_sum_ref[:, t * width : (t + 1) * width] = row
        weight = into_ref[:, t * width : (t + 1) * width].astype(F32)
        total = total + jnp.sum(row * weight, axis=1, keepdims=True)
    gain_a_sum_ref[...] = total.T / gain_a_ref[...].astype(F32)

    grads = jnp.concatenate(gathered(lines), axis=1)
    out_sum_ref[...] = grads[:part]
    total = jnp.zeros((part, 1), F32)
    for t in range(3):
        row = grads[(1 + t) * part : (2 + t) * part]
        expand_sum_ref[:, t * width : (t + 1) * width] = row
        weight = expand_ref[:, t * width : (t + 1) * width].astype(F32)
        total = total + jnp.sum(row * weight, axis=1, keepdims=True)
    gain_b_sum_ref[...] = total.T / gain_b_ref[...].astype(F32)
    contract_sum_ref[...] = grads[4 * part : 4 * part + held]


def finish(where, mine, other, projection_in, expansion, gain_a, gain_b, held):
    part, wide = projection_in.shape
    inside = pl.BlockSpec(memory_space=pltpu.VMEM)
    shapes = [(part, wide), (1, part), (part, wide // 3), (part, wide), (1, part), (held, wide // 3)]
    return pl.pallas_call(
        finish_kernel,
        in_specs=[pl.BlockSpec(memory_space=pltpu.SMEM)] + [inside] * 6,
        out_specs=[inside] * 6,
        out_shape=[jax.ShapeDtypeStruct(shape, F32) for shape in shapes],
        compiler_params=pltpu.CompilerParams(vmem_limit_bytes=20 * 2**20),
        name="finish",
    )(where, mine, other, projection_in, expansion, gain_a[None], gain_b[None])


def local(size, ranks, tokens, gain_a, projection_in, attention_out, gain_b, expansion, contraction, cotangent):
    z = lax.axis_index("fsdp")
    r = lax.axis_index("rep")
    core = r & 1
    group = 2 * core + (z & 1)
    home = core == z >> 1
    own = tokens[0]
    count, width = own.shape
    part = width // size
    hidden = contraction.shape[0]
    heads = HEADS // size

    stages = list(range(len(far(ranks))))
    where = jnp.stack([z, core]).astype(jnp.int32)
    columns = [projection_in[:, t * width : (t + 1) * width] for t in range(3)]
    piece = split_rows(jnp.concatenate(columns, axis=0), r, ranks)
    rows = piece.shape[0]
    gains = jnp.pad(jnp.concatenate([gain_a, gain_b])[None], ((0, 7), (0, width - 2 * part)))
    pieces = jnp.stack(exchange([jnp.concatenate([piece, gains], axis=0)] * size, size))
    gains = reorder(pieces[:, rows, : 2 * part], z, size).astype(F32)
    gain_one = gains[:, :part].reshape(1, width)
    gain_two = gains[:, part:].reshape(1, width)
    freqs = THETA ** (-(jnp.arange(HALF, dtype=F32) * (2.0 / HEAD_DIM)))
    places = jnp.concatenate([(group ^ d) * count + jnp.arange(count, dtype=jnp.int32) for d in range(size)])
    angles = freqs[:, None] * places.astype(F32)[None, :]
    early = (gain_one, gain_two, jnp.cos(angles), jnp.sin(angles))
    pair, other, first, second, early = collect(own, home, size, ranks, early)
    gain_one, gain_two, cosine, sine = early
    into = grow(pieces[:, :rows], r, ranks, stages[:-1])
    into = grow(after(into, first), r, ranks, stages[-1:])
    into_other = swap(into, "rep", ranks, 1)
    normed, queries, keys, values = project(
        where, pair, other, gain_one, cosine, sine, into, into_other, count
    )

    columns = [expansion[:, t * width : (t + 1) * width] for t in range(3)]
    stacked = jnp.concatenate([attention_out] + columns + [contraction], axis=0)
    pad = -stacked.shape[0] % max(32, 8 * ranks)
    stacked = jnp.concatenate([stacked, jnp.zeros((pad, width), BF16)], axis=0)
    rest = exchange([split_rows(after(stacked, second), r, ranks)] * size, size)
    merged = []
    logs = []
    for head in range(heads):
        out, log = attend(head, queries, after(keys, *merged[-1:]), values)
        merged.append(out)
        logs.append(log)
    rest = jnp.stack(after(rest, merged[0]))
    for stage in stages[:-1]:
        rest = join(rest, after(stage_swap(rest, ranks, stage), merged[-1]), stage_upper(r, ranks, stage))
    own_merged = jnp.concatenate(merged, axis=0)
    merged = trade_out([own_merged[:, d * count : (d + 1) * count] for d in range(size)], size, ranks)
    coming = after(stage_swap(rest, ranks, stages[-1]), *merged)
    rest = join(rest, coming, stage_upper(r, ranks, stages[-1]))
    rest_other = swap(rest, "rep", ranks, 1)
    upstream = cotangent[0]
    block_output, state_back, state_low, normed_two, active, inner_back, *merged_back = forward_back(
        where, merged, own, upstream, gain_two, [rest, rest_other], size * hidden
    )
    arrived = trade_back(merged_back, size, ranks)
    own_upstream = arrived

    kept, sent = gradients(
        where, merged, upstream, state_low, normed_two, active, inner_back, stacked.shape[0]
    )
    sent = after(sent, *arrived[:3])
    other = swap(sent, "rep", ranks, 1)
    upper = stage_upper(r, ranks, stages[-1])
    (sent, kept), (other_sent, other) = cut(kept, upper), cut(other, upper)
    sent = add(sent, other_sent)

    turned_backs = []
    weight_backs = []
    received = []
    ahead = [sent]
    for head in range(heads):
        grad, weight_grad = attend_back(
            head, queries, keys, values, after(own_upstream, *ahead), own_merged, logs[head],
            cosine, sine, normed,
        )
        turned_backs.append(grad)
        weight_backs.append(weight_grad.reshape(3, HEAD_DIM, width))
        received.append(trade_out([grad[:, d * count : (d + 1) * count] for d in range(size)], size, ranks))
        if head == 0:
            coming = stage_swap(sent, ranks, stages[-1])
            grads = (kept.astype(F32) + other.astype(F32) + coming.astype(F32)).astype(BF16)
            grads = shrink(grads, r, ranks, stages[-2:0:-1])
            ahead = [grads]
        if head == 1:
            grads = shrink(grads, r, ranks, stages[:1])
            ahead = [grads] + received[0]

    sent, kept = [jnp.stack([pick(grads, bit), pick(grads, bit + 2)]) for bit in (z & 1 ^ 1, z & 1)]
    grads = add(kept, swap(sent, "fsdp", size, 1))
    weight_backs[2], grads = after((weight_backs[2], grads), turned_backs[2], *received[1][:2])
    into_grad = jnp.concatenate([grad[t] for t in range(3) for grad in weight_backs], axis=0)
    later, last = received[1:]
    into_grad = after(shrink(into_grad[None], r, ranks, stages[-1:]), later[2], last[0])
    into_grad = after(shrink(into_grad, r, ranks, stages[-2::-1]), later[3], last[1])[0]
    grads = add(pick(grads, z >> 1), swap(pick(grads, z >> 1 ^ 1), "fsdp", size, 2))
    lines = into_grad.shape[0]
    blocks = into_grad.reshape(lines, size, part).transpose(1, 0, 2)
    blocks = exchange([pick(blocks, z ^ d) for d in range(size)], size)
    even, odd = (blocks[0].astype(F32) + blocks[2].astype(F32)), (blocks[1].astype(F32) + blocks[3].astype(F32))
    low = z & 1 == 0
    flat = jnp.concatenate([jnp.where(low, even, odd), jnp.where(low, odd, even)], axis=1).astype(BF16)
    both = grow_flat(jnp.concatenate([flat, grads], axis=0)[None], r, ranks, stages[:-1])
    both = grow_flat(after(both, *last[2:]), r, ranks, stages[-1:])
    token_grad = token_back(where, received, into, into_other, own, state_back, gain_one)[None]
    both = after(both, token_grad)
    into_sum, gain_one_sum, attention_out_sum, expansion_sum, gain_two_sum, contraction_sum = finish(
        where, both, swap(both, "rep", ranks, 1), projection_in, expansion, gain_a, gain_b, hidden
    )
    return (
        block_output[None],
        token_grad,
        gain_one_sum[0],
        into_sum,
        attention_out_sum,
        gain_two_sum[0],
        expansion_sum,
        contraction_sum,
    )


def solution(mesh):
    tokens, rows, line = P("rep", "fsdp", None), P("fsdp", None), P("fsdp")
    in_specs = (tokens, line, rows, rows, line, rows, rows, tokens)
    out_specs = (tokens, tokens, line, rows, rows, line, rows, rows)
    body = functools.partial(local, mesh.shape["fsdp"], mesh.shape["rep"])
    return jax.shard_map(body, mesh=mesh, in_specs=in_specs, out_specs=out_specs, check_vma=False)
```

profile of v0, /device:TPU:1, one launch (start us, length us, event | category | flops | bytes accessed | tf_op | source)
XLA Modules:
  0.0 297.4 jit_solution(3310521281489563503)
XLA Ops:
  0.7 1.3 fusion.11
  2.2 2.2 collective-permute-start.2
  4.4 2.3 collective-permute-start.3
  6.7 2.7 collective-permute-start
  9.5 5.2 %collective-permute-done.4 = bf16[80,768]{1,0:T(8,128)(2,1)S(1)} collective-permute-done((bf16[80,768]{1,0:T(8,128)(2,1)S(1)}, bf16[80,768]{1,0:T(8,128)(2,1)S(1)}, u32[]{:S(2)}, u32[]{:S(2)}) %collective-permute-start.4) | collective-permute-done | bytes 122912 | tf_op jit(solution)/shard_map/ppermute | solution.py:438
  14.7 1.3 collective-permute-start.6
  16.0 6.2 %collective-permute-done.6 = bf16[4,72,768]{2,1,0:T(8,128)(2,1)S(1)} collective-permute-done((bf16[4,72,768]{2,1,0:T(8,128)(2,1)S(1)}, bf16[4,72,768]{2,1,0:T(8,128)(2,1)S(1)}, u32[]{:S(2)}, u32[]{:S(2)}) %collective-permute-start.6) | collective-permute-done | bytes 442400 | tf_op jit(solution)/shard_map/ppermute | solution.py:504
  22.4 12.7 %collective-permute-done = bf16[512,768]{1,0:T(8,128)(2,1)S(1)} collective-permute-done((bf16[512,768]{1,0:T(8,128)(2,1)S(1)}, bf16[512,768]{1,0:T(8,128)(2,1)S(1)}, u32[]{:S(2)}, u32[]{:S(2)}) %collective-permute-start) | collective-permute-done | bytes 786464 | tf_op jit(solution)/shard_map/ppermute | solution.py:452
  38.3 1.9 collective-permute-start.1
  40.5 7.5 %collective-permute-done.7 = bf16[4,144,768]{2,1,0:T(8,128)(2,1)} collective-permute-done((bf16[4,144,768]{2,1,0:T(8,128)(2,1)S(1)}, bf16[4,144,768]{2,1,0:T(8,128)(2,1)}, u32[]{:S(2)}, u32[]{:S(2)}) %collective-permute-start.7) | collective-permute-done | bytes 884768 | tf_op jit(solution)/shard_map/ppermute | solution.py:504
  48.0 1.4 broadcast_select_fusion.3
  49.6 1.7 collective-permute-done.1
  51.3 1.3 broadcast_select_fusion.7
  55.3 4.6 %collective-permute-start.14 = (bf16[136,768]{1,0:T(8,128)(2,1)S(1)}, bf16[136,768]{1,0:T(8,128)(2,1)S(1)}, u32[]{:S(2)}, u32[]{:S(2)}) collective-permute-start(bf16[136,768]{1,0:T(8,128)(2,1)S(1)} %constant_dynamic-slice_fusion.10), channel_id=1, source_target_pairs={{0,16},{8,24},{16,0},{24,8},{1,17},{9,25},{17,1},{25,9},{2,18},{10... | collective-permute-start | bytes 626696 | tf_op jit(solution)/shard_map/ppermute | solution.py:438
  59.9 10.5 %project.1 = (bf16[2048,768]{1,0:T(8,128)(2,1)S(1)}, bf16[192,2048]{1,0:T(8,128)(2,1)S(1)}, bf16[192,2048]{1,0:T(8,128)(2,1)S(1)}, bf16[192,2048]{1,0:T(8,128)(2,1)S(1)}) custom-call(s32[2]{0:T(128)S(1)} %pad_add_fusion.place_ref, bf16[1024,768]{1,0:T(8,128)(2,1)} %pad_maximum_fusion.3.pair_ref, bf16[1024,768]{1,0:T(8,128)(2,1)} %collective-permute-done.5.other_ref, ...), custom_call_target="tpu_custom_call" | custom-call | flops 8000000000 | bytes 20000000 | tf_op jit(solution)/shard_map/project/pallas_call | solution.py:221
  70.4 1.7 copy-done.33
  72.1 6.1 %attend.3 = (bf16[64,2048]{1,0:T(8,128)(2,1)S(1)}, f32[1,2048]{1,0:T(1,128)S(1)}) custom-call(bf16[192,2048]{1,0:T(8,128)(2,1)S(1)} %get-tuple-element.81.q_ref, bf16[192,2048]{1,0:T(8,128)(2,1)S(1)} %get-tuple-element.87.k_ref.kt_ref, bf16[192,2048]{1,0:T(8,128)(2,1)S(1)} %get-tuple-element.83.v_ref.vt_ref), custom_call_target="tpu_custom_call" | custom-call | flops 7516192768 | bytes 1048576 | tf_op jit(solution)/shard_map/attend/pallas_call | solution.py:43
  78.7 6.1 %attend.4 = (bf16[64,2048]{1,0:T(8,128)(2,1)S(1)}, f32[1,2048]{1,0:T(1,128)S(1)}) custom-call(bf16[192,2048]{1,0:T(8,128)(2,1)S(1)} %get-tuple-element.81.q_ref, bf16[192,2048]{1,0:T(8,128)(2,1)S(1)} %get-tuple-element.87.k_ref.kt_ref, bf16[192,2048]{1,0:T(8,128)(2,1)S(1)} %get-tuple-element.83.v_ref.vt_ref), custom_call_target="tpu_custom_call" | custom-call | flops 7516192768 | bytes 1048576 | tf_op jit(solution)/shard_map/attend/pallas_call | solution.py:43
  84.8 6.1 %attend.5 = (bf16[64,2048]{1,0:T(8,128)(2,1)S(1)}, f32[1,2048]{1,0:T(1,128)S(1)}) custom-call(bf16[192,2048]{1,0:T(8,128)(2,1)S(1)} %get-tuple-element.81.q_ref, bf16[192,2048]{1,0:T(8,128)(2,1)S(1)} %get-tuple-element.87.k_ref.kt_ref, bf16[192,2048]{1,0:T(8,128)(2,1)S(1)} %get-tuple-element.83.v_ref.vt_ref), custom_call_target="tpu_custom_call" | custom-call | flops 7516192768 | bytes 1048576 | tf_op jit(solution)/shard_map/attend/pallas_call | solution.py:43
  91.2 1.3 collective-permute-start.17
  92.7 4.6 %collective-permute-start.10 = (bf16[192,512]{1,0:T(8,128)(2,1)S(1)}, bf16[192,512]{1,0:T(8,128)(2,1)S(1)}, u32[]{:S(2)}, u32[]{:S(2)}) collective-permute-start(bf16[192,512]{1,0:T(8,128)(2,1)S(1)} %get-tuple-element.175), channel_id=1, source_target_pairs={{0,8},{1,24},{2,10},{3,26},{4,12},{5,28},{6,14},{7,30},{8,0},{9,16... | collective-permute-start | bytes 589832 | tf_op jit(solution)/shard_map/ppermute | solution.py:452
  97.9 2.8 collective-permute-start.9
  100.7 2.2 collective-permute-done.10.m1_ref
  102.9 8.3 %collective-permute-done.11.m2_ref = bf16[192,512]{1,0:T(8,128)(2,1)S(1)} collective-permute-done((bf16[192,512]{1,0:T(8,128)(2,1)S(1)}, bf16[192,512]{1,0:T(8,128)(2,1)S(1)}, u32[]{:S(2)}, u32[]{:S(2)}) %collective-permute-start.11) | collective-permute-done | bytes 196640 | tf_op jit(solution)/shard_map/ppermute | solution.py:452
  113.1 2.5 collective-permute-start.18
  115.6 5.6 %collective-permute-done.18.theirs_ref = bf16[4,544,768]{2,1,0:T(8,128)(2,1)S(1)} collective-permute-done((bf16[4,544,768]{2,1,0:T(8,128)(2,1)S(1)}, bf16[4,544,768]{2,1,0:T(8,128)(2,1)S(1)}, u32[]{:S(2)}, u32[]{:S(2)}) %collective-permute-start.18) | collective-permute-done | bytes 3342368 | tf_op jit(solution)/shard_map/ppermute | solution.py:438
  121.2 13.1 %forward_back.1 = (bf16[512,768]{1,0:T(8,128)(2,1)}, f32[512,768]{1,0:T(8,128)S(1)}, bf16[512,768]{1,0:T(8,128)(2,1)S(1)}, bf16[512,768]{1,0:T(8,128)(2,1)S(1)},...) custom-call(s32[2]{0:T(128)S(1)} %pad_add_fusion.place_ref, ...), custom_call_target="tpu_custom_call" | custom-call | flops 14000000000 | bytes 20000000 | tf_op jit(solution)/shard_map/forward_back/pallas_call | solution.py:326
  134.2 4.1 %collective-permute-start.19 = (bf16[192,512]{1,0:T(8,128)(2,1)S(1)}, bf16[192,512]{1,0:T(8,128)(2,1)S(1)}, u32[]{:S(2)}, u32[]{:S(2)}) collective-permute-start(bf16[192,512]{1,0:T(8,128)(2,1)S(1)} %get-tuple-element.98), channel_id=1, source_target_pairs={{0,0},{1,16},{2,2},{3,18},{4,4},{5,20},{6,6},{7,22},{8,8},{9,24},{... | collective-permute-start | bytes 589832 | tf_op jit(solution)/shard_map/ppermute | solution.py:452
  138.3 1.7 collective-permute-start.20
  140.0 5.2 %gradients.1 = (bf16[4,1088,384]{2,1,0:T(8,128)(2,1)S(1)}, bf16[4,1088,384]{2,1,0:T(8,128)(2,1)}) custom-call(s32[2]{0:T(128)S(1)} %pad_add_fusion.place_ref, bf16[192,512]{1,0:T(8,128)(2,1)S(1)} %collective-permute-done.9.m0_ref, bf16[192,512]{1,0:T(8,128)(2,1)S(1)} %collective-permute-done.10.m1_ref, bf16[192,512]{1,0:T(8,128)(2,1)S(1)} %collective-permute-done.11.m2_ref, ...), custom_call_target="tpu_custom_call" | custom-call | flops 12000000000 | bytes 12000000 | tf_op jit(solution)/shard_map/gradients/pallas_call | solution.py:369
  145.3 1.7 copy-done.2
  147.0 1.5 collective-permute-done.19.u0_ref
  150.5 3.5 %collective-permute-start.23 = (bf16[4,1088,384]{2,1,0:T(8,128)(2,1)}, bf16[4,1088,384]{2,1,0:T(8,128)(2,1)}, u32[]{:S(2)}, u32[]{:S(2)}) collective-permute-start(bf16[4,1088,384]{2,1,0:T(8,128)(2,1)} %get-tuple-element.108), channel_id=1, source_target_pairs={{0,1},{1,0},{2,3},{3,2},{4,5},{5,4},{6,7},{7,6},{8,9},{9,8},{10,11... | collective-permute-start | bytes 10027016 | tf_op jit(solution)/shard_map/ppermute | solution.py:438
  154.1 2.6 collective-permute-start.22
  156.6 3.4 %collective-permute-done.23 = bf16[4,1088,384]{2,1,0:T(8,128)(2,1)} collective-permute-done((bf16[4,1088,384]{2,1,0:T(8,128)(2,1)}, bf16[4,1088,384]{2,1,0:T(8,128)(2,1)}, u32[]{:S(2)}, u32[]{:S(2)}) %collective-permute-start.23) | collective-permute-done | bytes 3342368 | tf_op jit(solution)/shard_map/ppermute | solution.py:438
  160.0 2.5 add_convert_fusion.1
  166.6 13.5 %attend_back.3 = (bf16[192,2048]{1,0:T(8,128)(2,1)S(1)}, bf16[192,768]{1,0:T(8,128)(2,1)S(1)}) custom-call(bf16[192,2048]{1,0:T(8,128)(2,1)S(1)} %copy-done.36, bf16[192,2048]{1,0:T(8,128)(2,1)S(1)} %copy-done.39, bf16[192,2048]{1,0:T(8,128)(2,1)S(1)} %copy-done.42, bf16[192,512]{1,0:T(8,128)(2,1)S(1)} %copy-done.26, bf16[192,512]{1,0:T(8,128)(2,1)S(1)} %copy-done.28, ...), custom_call_target="tpu_custom_call" | custom-call | flops 15032385536 | bytes 2097152 | tf_op jit(solution)/shard_map/attend_back/pallas_call | solution.py:113
  180.2 2.8 collective-permute-start.24
  183.0 1.8 collective-permute-start.25
  184.9 2.3 collective-permute-start.27
  187.2 2.2 add_convert_fusion
  190.7 13.3 %attend_back.4 = (bf16[192,2048]{1,0:T(8,128)(2,1)S(1)}, bf16[192,768]{1,0:T(8,128)(2,1)S(1)}) custom-call(bf16[192,2048]{1,0:T(8,128)(2,1)S(1)} %copy-done.37, bf16[192,2048]{1,0:T(8,128)(2,1)S(1)} %copy-done.40, bf16[192,2048]{1,0:T(8,128)(2,1)S(1)} %copy-done.43, bf16[192,512]{1,0:T(8,128)(2,1)S(1)} %copy-done.26, bf16[192,512]{1,0:T(8,128)(2,1)S(1)} %copy-done.28, ...), custom_call_target="tpu_custom_call" | custom-call | flops 15032385536 | bytes 2097152 | tf_op jit(solution)/shard_map/attend_back/pallas_call | solution.py:113
  204.9 2.7 collective-permute-start.29
  208.8 2.8 collective-permute-start.30
  212.3 13.5 %attend_back.5 = (bf16[192,2048]{1,0:T(8,128)(2,1)S(1)}, bf16[192,768]{1,0:T(8,128)(2,1)S(1)}) custom-call(bf16[192,2048]{1,0:T(8,128)(2,1)S(1)} %copy-done.37, bf16[192,2048]{1,0:T(8,128)(2,1)S(1)} %copy-done.40, bf16[192,2048]{1,0:T(8,128)(2,1)S(1)} %copy-done.43, bf16[192,512]{1,0:T(8,128)(2,1)S(1)} %copy-done.26, bf16[192,512]{1,0:T(8,128)(2,1)S(1)} %copy-done.28, ...), custom_call_target="tpu_custom_call" | custom-call | flops 15032385536 | bytes 2097152 | tf_op jit(solution)/shard_map/attend_back/pallas_call | solution.py:113
  228.9 2.1 fusion.12
  231.0 4.3 %collective-permute-start.34 = (bf16[192,512]{1,0:T(8,128)(2,1)S(1)}, bf16[192,512]{1,0:T(8,128)(2,1)S(1)}, u32[]{:S(2)}, u32[]{:S(2)}) collective-permute-start(bf16[192,512]{1,0:T(8,128)(2,1)S(1)} %get-tuple-element.164), channel_id=1, source_target_pairs={{0,0},{1,16},{2,2},{3,18},{4,4},{5,20},{6,6},{7,22},{8,8},{9,24},{... | collective-permute-start | bytes 589832 | tf_op jit(solution)/shard_map/ppermute | solution.py:452
  236.6 4.4 %collective-permute-done.34.refs_8_ = bf16[192,512]{1,0:T(8,128)(2,1)S(1)} collective-permute-done((bf16[192,512]{1,0:T(8,128)(2,1)S(1)}, bf16[192,512]{1,0:T(8,128)(2,1)S(1)}, u32[]{:S(2)}, u32[]{:S(2)}) %collective-permute-start.34) | collective-permute-done | bytes 196640 | tf_op jit(solution)/shard_map/ppermute | solution.py:452
  242.8 3.1 %collective-permute-start.35 = (bf16[192,512]{1,0:T(8,128)(2,1)}, bf16[192,512]{1,0:T(8,128)(2,1)S(1)}, u32[]{:S(2)}, u32[]{:S(2)}) collective-permute-start(bf16[192,512]{1,0:T(8,128)(2,1)} %get-tuple-element.163), channel_id=1, source_target_pairs={{0,8},{1,24},{2,10},{3,26},{4,12},{5,28},{6,14},{7,30},{8,0},{9,16... | collective-permute-start | bytes 589832 | tf_op jit(solution)/shard_map/ppermute | solution.py:452
  245.9 1.6 dynamic-slice_bitcast_fusion.1
  248.0 1.8 add_convert_fusion.4
  249.8 1.6 collective-permute-done.32.refs_7_
  251.4 4.4 %collective-permute-done.35.refs_9_ = bf16[192,512]{1,0:T(8,128)(2,1)S(1)} collective-permute-done((bf16[192,512]{1,0:T(8,128)(2,1)}, bf16[192,512]{1,0:T(8,128)(2,1)S(1)}, u32[]{:S(2)}, u32[]{:S(2)}) %collective-permute-start.35) | collective-permute-done | bytes 196640 | tf_op jit(solution)/shard_map/ppermute | solution.py:452
  255.8 1.9 reshape_squeeze.3
  257.7 2.3 constant_dynamic-slice_fusion.3
  260.2 3.6 %collective-permute-start.43 = (bf16[144,192]{1,0:T(8,128)(2,1)S(1)}, bf16[144,192]{1,0:T(8,128)(2,1)S(1)}, u32[]{:S(2)}, u32[]{:S(2)}) collective-permute-start(bf16[144,192]{1,0:T(8,128)(2,1)S(1)} %bitcast.90), channel_id=1, source_target_pairs={{0,24},{8,16},{16,8},{24,0},{1,25},{9,17},{17,9},{25,1},{2,26},{10... | collective-permute-start | bytes 165896 | tf_op jit(solution)/shard_map/ppermute | solution.py:438
  264.8 2.1 collective-permute-done.43
  267.6 3.5 %collective-permute-start.36 = (bf16[192,512]{1,0:T(8,128)(2,1)S(1)}, bf16[192,512]{1,0:T(8,128)(2,1)S(1)}, u32[]{:S(2)}, u32[]{:S(2)}) collective-permute-start(bf16[192,512]{1,0:T(8,128)(2,1)S(1)} %copy-done.52), channel_id=1, source_target_pairs={{0,16},{1,0},{2,18},{3,2},{4,20},{5,4},{6,22},{7,6},{8,24},{9,8},{... | collective-permute-start | bytes 589832 | tf_op jit(solution)/shard_map/ppermute | solution.py:452
  271.2 3.4 %collective-permute-start.37 = (bf16[192,512]{1,0:T(8,128)(2,1)S(1)}, bf16[192,512]{1,0:T(8,128)(2,1)S(1)}, u32[]{:S(2)}, u32[]{:S(2)}) collective-permute-start(bf16[192,512]{1,0:T(8,128)(2,1)S(1)} %copy-done.51), channel_id=1, source_target_pairs={{0,24},{1,8},{2,26},{3,10},{4,28},{5,12},{6,30},{7,14},{8,16},{9,0... | collective-permute-start | bytes 589832 | tf_op jit(solution)/shard_map/ppermute | solution.py:452
  275.3 4.3 %collective-permute-done.37.refs_11_ = bf16[192,512]{1,0:T(8,128)(2,1)S(1)} collective-permute-done((bf16[192,512]{1,0:T(8,128)(2,1)S(1)}, bf16[192,512]{1,0:T(8,128)(2,1)S(1)}, u32[]{:S(2)}, u32[]{:S(2)}) %collective-permute-start.37) | collective-permute-done | bytes 196640 | tf_op jit(solution)/shard_map/ppermute | solution.py:452
  280.0 7.0 %token_back.1 = f32[512,768]{1,0:T(8,128)} custom-call(s32[2]{0:T(128)S(1)} %pad_add_fusion.place_ref, bf16[192,512]{1,0:T(8,128)(2,1)S(1)} %copy-done.14, bf16[192,512]{1,0:T(8,128)(2,1)S(1)} %copy-done.16, bf16[192,512]{1,0:T(8,128)(2,1)S(1)} %copy-done.18, bf16[192,512]{1,0:T(8,128)(2,1)S(1)} %copy-done.20, bf16[192,512]{1,0:T(8,128)(2,1)S(1)} %copy-done.22, ...), custom_call_target="tpu_custom_call" | custom-call | flops 5000000000 | bytes 12000000 | tf_op jit(solution)/shard_map/token_back/pallas_call | solution.py:414
  287.1 2.0 collective-permute-done.46
  290.4 2.6 collective-permute-done.47.other_ref
  293.0 4.2 %finish.1 = (f32[192,2304]{1,0:T(8,128)}, f32[1,192]{1,0:T(1,128)}, f32[192,768]{1,0:T(8,128)}, f32[192,2304]{1,0:T(8,128)}, f32[1,192]{1,0:T(1,128)}, /*index=5*/f32[288,768]{1,0:T(8,128)}) custom-call(s32[2]{0:T(128)S(1)} %pad_add_fusion.place_ref, bf16[4,416,384]{2,1,0:T(8,128)(2,1)S(1)} %pad_maximum_fusion.4.mine_ref, ...), custom_call_target="tpu_custom_call" | custom-call | tf_op jit(solution)/shard_map/finish/pallas_call | solution.py:614
  (231 shorter events, 31.1 us)
Async XLA Ops:
  2.2 7.3 %collective-permute-start.2 = (bf16[80,768]{1,0:T(8,128)(2,1)S(1)}, bf16[80,768]{1,0:T(8,128)(2,1)S(1)}, u32[]{:S(2)}, u32[]{:S(2)}) collective-permute-start(bf16[80,768]{1,0:T(8,128)(2,1)S(1)} %get-tuple-element.188), channel_id=1, source_target_pairs={{0,8},{8,0},{16,24},{24,16},{1,9},{9,1},{17,25},{25,17},{2,10},{10... | collective-permute-start | bytes 368648 | tf_op jit(solution)/shard_map/ppermute | solution.py:438
  4.4 5.1 %collective-permute-start.3 = (bf16[80,768]{1,0:T(8,128)(2,1)S(1)}, bf16[80,768]{1,0:T(8,128)(2,1)S(1)}, u32[]{:S(2)}, u32[]{:S(2)}) collective-permute-start(bf16[80,768]{1,0:T(8,128)(2,1)S(1)} %get-tuple-element.188), channel_id=1, source_target_pairs={{0,16},{8,24},{16,0},{24,8},{1,17},{9,25},{17,1},{25,9},{2,18},{10... | collective-permute-start | bytes 368648 | tf_op jit(solution)/shard_map/ppermute | solution.py:438
  6.7 7.9 %collective-permute-start.4 = (bf16[80,768]{1,0:T(8,128)(2,1)S(1)}, bf16[80,768]{1,0:T(8,128)(2,1)S(1)}, u32[]{:S(2)}, u32[]{:S(2)}) collective-permute-start(bf16[80,768]{1,0:T(8,128)(2,1)S(1)} %get-tuple-element.188), channel_id=1, source_target_pairs={{0,24},{8,16},{16,8},{24,0},{1,25},{9,17},{17,9},{25,1},{2,26},{10... | collective-permute-start | bytes 368648 | tf_op jit(solution)/shard_map/ppermute | solution.py:438
  6.7 28.4 %collective-permute-start = (bf16[512,768]{1,0:T(8,128)(2,1)S(1)}, bf16[512,768]{1,0:T(8,128)(2,1)S(1)}, u32[]{:S(2)}, u32[]{:S(2)}) collective-permute-start(bf16[512,768]{1,0:T(8,128)(2,1)S(1)} %bitcast.63), channel_id=1, source_target_pairs={{0,8},{1,16},{2,10},{3,18},{4,12},{5,20},{6,14},{7,22},{8,0},{9,24... | collective-permute-start | bytes 2359304 | tf_op jit(solution)/shard_map/ppermute | solution.py:452
  14.7 7.5 %collective-permute-start.6 = (bf16[4,72,768]{2,1,0:T(8,128)(2,1)S(1)}, bf16[4,72,768]{2,1,0:T(8,128)(2,1)S(1)}, u32[]{:S(2)}, u32[]{:S(2)}) collective-permute-start(bf16[4,72,768]{2,1,0:T(8,128)(2,1)S(1)} %pad_maximum_fusion.8), channel_id=1, source_target_pairs={{0,2},{1,5},{2,0},{3,7},{4,6},{5,1},{6,4},{7,3},{8,10},{9,13},{10,... | collective-permute-start | bytes 1327112 | tf_op jit(solution)/shard_map/ppermute | solution.py:504
  36.0 12.0 %collective-permute-start.7 = (bf16[4,144,768]{2,1,0:T(8,128)(2,1)S(1)}, bf16[4,144,768]{2,1,0:T(8,128)(2,1)}, u32[]{:S(2)}, u32[]{:S(2)}) collective-permute-start(bf16[4,144,768]{2,1,0:T(8,128)(2,1)S(1)} %pad_maximum_fusion.5), channel_id=1, source_target_pairs={{0,4},{1,3},{2,6},{3,1},{4,0},{5,7},{6,2},{7,5},{8,12},{9,11},{10,... | collective-permute-start | bytes 2654216 | tf_op jit(solution)/shard_map/ppermute | solution.py:504
  38.2 21.7 %copy-start.8 = (f32[32,2048]{1,0:T(8,128)}, f32[32,2048]{1,0:T(8,128)S(1)}, u32[]{:S(2)}) copy-start(f32[32,2048]{1,0:T(8,128)S(1)} %get-tuple-element.79.sin_ref) | copy-start | bytes 786436
  38.2 21.7 %copy-start.10 = (f32[32,2048]{1,0:T(8,128)}, f32[32,2048]{1,0:T(8,128)S(1)}, u32[]{:S(2)}) copy-start(f32[32,2048]{1,0:T(8,128)S(1)} %get-tuple-element.78.cos_ref) | copy-start | bytes 786436
  38.3 13.1 %collective-permute-start.1 = (bf16[512,768]{1,0:T(8,128)(2,1)}, bf16[512,768]{1,0:T(8,128)(2,1)}, u32[]{:S(2)}, u32[]{:S(2)}) collective-permute-start(bf16[512,768]{1,0:T(8,128)(2,1)} %copy-done.48), channel_id=1, source_target_pairs={{1,9},{3,11},{5,13},{7,15},{9,1},{11,3},{13,5},{15,7},{16,24},{18,... | collective-permute-start | bytes 2359304 | tf_op jit(solution)/shard_map/ppermute | solution.py:452
  49.6 10.3 %collective-permute-start.8 = (bf16[4,288,768]{2,1,0:T(8,128)(2,1)S(1)}, bf16[4,288,768]{2,1,0:T(8,128)(2,1)}, u32[]{:S(2)}, u32[]{:S(2)}) collective-permute-start(bf16[4,288,768]{2,1,0:T(8,128)(2,1)S(1)} %pad_maximum_fusion.1.mine_ref.refs_12_), channel_id=1, source_target_pairs={{0,1},{1,0},{2,3},{3,2},{4,5},{5,4},{6,7},{7,6},{8,9},{9,8},{10,11... | collective-permute-start | bytes 5308424 | tf_op jit(solution)/shard_map/ppermute | solution.py:438
  53.9 6.0 %collective-permute-start.5 = (bf16[1024,768]{1,0:T(8,128)(2,1)}, bf16[1024,768]{1,0:T(8,128)(2,1)}, u32[]{:S(2)}, u32[]{:S(2)}) collective-permute-start(bf16[1024,768]{1,0:T(8,128)(2,1)} %pad_maximum_fusion.3.pair_ref), channel_id=1, source_target_pairs={{0,1},{1,0},{2,3},{3,2},{4,5},{5,4},{6,7},{7,6},{8,9},{9,8},{10,11... | collective-permute-start | bytes 4718600 | tf_op jit(solution)/shard_map/ppermute | solution.py:438
  55.2 23.0 %collective-permute-start.13 = (bf16[136,768]{1,0:T(8,128)(2,1)S(1)}, bf16[136,768]{1,0:T(8,128)(2,1)S(1)}, u32[]{:S(2)}, u32[]{:S(2)}) collective-permute-start(bf16[136,768]{1,0:T(8,128)(2,1)S(1)} %constant_dynamic-slice_fusion.10), channel_id=1, source_target_pairs={{0,8},{8,0},{16,24},{24,16},{1,9},{9,1},{17,25},{25,17},{2,10},{10... | collective-permute-start | bytes 626696 | tf_op jit(solution)/shard_map/ppermute | solution.py:438
  55.3 23.0 %collective-permute-start.14 = (bf16[136,768]{1,0:T(8,128)(2,1)S(1)}, bf16[136,768]{1,0:T(8,128)(2,1)S(1)}, u32[]{:S(2)}, u32[]{:S(2)}) collective-permute-start(bf16[136,768]{1,0:T(8,128)(2,1)S(1)} %constant_dynamic-slice_fusion.10), channel_id=1, source_target_pairs={{0,16},{8,24},{16,0},{24,8},{1,17},{9,25},{17,1},{25,9},{2,18},{10... | collective-permute-start | bytes 626696 | tf_op jit(solution)/shard_map/ppermute | solution.py:438
  59.9 18.4 %collective-permute-start.15 = (bf16[136,768]{1,0:T(8,128)(2,1)S(1)}, bf16[136,768]{1,0:T(8,128)(2,1)S(1)}, u32[]{:S(2)}, u32[]{:S(2)}) collective-permute-start(bf16[136,768]{1,0:T(8,128)(2,1)S(1)} %constant_dynamic-slice_fusion.10), channel_id=1, source_target_pairs={{0,24},{8,16},{16,8},{24,0},{1,25},{9,17},{17,9},{25,1},{2,26},{10... | collective-permute-start | bytes 626696 | tf_op jit(solution)/shard_map/ppermute | solution.py:438
  72.1 12.7 %copy-start.38 = (bf16[192,2048]{1,0:T(8,128)(2,1)}, bf16[192,2048]{1,0:T(8,128)(2,1)S(1)}, u32[]{:S(2)}) copy-start(bf16[192,2048]{1,0:T(8,128)(2,1)S(1)} %get-tuple-element.87.k_ref.kt_ref) | copy-start | bytes 2359300
  72.1 12.7 %copy-start.41 = (bf16[192,2048]{1,0:T(8,128)(2,1)}, bf16[192,2048]{1,0:T(8,128)(2,1)S(1)}, u32[]{:S(2)}) copy-start(bf16[192,2048]{1,0:T(8,128)(2,1)S(1)} %get-tuple-element.83.v_ref.vt_ref) | copy-start | bytes 2359300
  78.4 12.5 %collective-permute-start.16 = (bf16[4,136,768]{2,1,0:T(8,128)(2,1)S(1)}, bf16[4,136,768]{2,1,0:T(8,128)(2,1)S(1)}, u32[]{:S(2)}, u32[]{:S(2)}) collective-permute-start(bf16[4,136,768]{2,1,0:T(8,128)(2,1)S(1)} %pad_maximum_fusion.6), channel_id=1, source_target_pairs={{0,2},{1,5},{2,0},{3,7},{4,6},{5,1},{6,4},{7,3},{8,10},{9,13},{10,... | collective-permute-start | bytes 2506760 | tf_op jit(solution)/shard_map/ppermute | solution.py:504
  91.2 21.0 %collective-permute-start.17 = (bf16[4,272,768]{2,1,0:T(8,128)(2,1)S(1)}, bf16[4,272,768]{2,1,0:T(8,128)(2,1)S(1)}, u32[]{:S(2)}, u32[]{:S(2)}) collective-permute-start(bf16[4,272,768]{2,1,0:T(8,128)(2,1)S(1)} %pad_maximum_fusion.2), channel_id=1, source_target_pairs={{0,4},{1,3},{2,6},{3,1},{4,0},{5,7},{6,2},{7,5},{8,12},{9,11},{10,... | collective-permute-start | bytes 5013512 | tf_op jit(solution)/shard_map/ppermute | solution.py:504
  92.7 10.2 %collective-permute-start.10 = (bf16[192,512]{1,0:T(8,128)(2,1)S(1)}, bf16[192,512]{1,0:T(8,128)(2,1)S(1)}, u32[]{:S(2)}, u32[]{:S(2)}) collective-permute-start(bf16[192,512]{1,0:T(8,128)(2,1)S(1)} %get-tuple-element.175), channel_id=1, source_target_pairs={{0,8},{1,24},{2,10},{3,26},{4,12},{5,28},{6,14},{7,30},{8,0},{9,16... | collective-permute-start | bytes 589832 | tf_op jit(solution)/shard_map/ppermute | solution.py:452
  97.2 13.9 %collective-permute-start.11 = (bf16[192,512]{1,0:T(8,128)(2,1)S(1)}, bf16[192,512]{1,0:T(8,128)(2,1)S(1)}, u32[]{:S(2)}, u32[]{:S(2)}) collective-permute-start(bf16[192,512]{1,0:T(8,128)(2,1)S(1)} %get-tuple-element.174), channel_id=1, source_target_pairs={{0,16},{1,0},{2,18},{3,2},{4,20},{5,4},{6,22},{7,6},{8,24},{9,8},{... | collective-permute-start | bytes 589832 | tf_op jit(solution)/shard_map/ppermute | solution.py:452
  97.2 13.9 %collective-permute-start.12 = (bf16[192,512]{1,0:T(8,128)(2,1)S(1)}, bf16[192,512]{1,0:T(8,128)(2,1)S(1)}, u32[]{:S(2)}, u32[]{:S(2)}) collective-permute-start(bf16[192,512]{1,0:T(8,128)(2,1)S(1)} %get-tuple-element.173), channel_id=1, source_target_pairs={{0,24},{1,8},{2,26},{3,10},{4,28},{5,12},{6,30},{7,14},{8,16},{9,0... | collective-permute-start | bytes 589832 | tf_op jit(solution)/shard_map/ppermute | solution.py:452
  97.9 14.3 %collective-permute-start.9 = (bf16[192,512]{1,0:T(8,128)(2,1)S(1)}, bf16[192,512]{1,0:T(8,128)(2,1)S(1)}, u32[]{:S(2)}, u32[]{:S(2)}) collective-permute-start(bf16[192,512]{1,0:T(8,128)(2,1)S(1)} %get-tuple-element.176), channel_id=1, source_target_pairs={{0,0},{1,16},{2,2},{3,18},{4,4},{5,20},{6,6},{7,22},{8,8},{9,24},{... | collective-permute-start | bytes 589832 | tf_op jit(solution)/shard_map/ppermute | solution.py:452
  113.1 8.0 %collective-permute-start.18 = (bf16[4,544,768]{2,1,0:T(8,128)(2,1)S(1)}, bf16[4,544,768]{2,1,0:T(8,128)(2,1)S(1)}, u32[]{:S(2)}, u32[]{:S(2)}) collective-permute-start(bf16[4,544,768]{2,1,0:T(8,128)(2,1)S(1)} %pad_maximum_fusion.mine_ref), channel_id=1, source_target_pairs={{0,1},{1,0},{2,3},{3,2},{4,5},{5,4},{6,7},{7,6},{8,9},{9,8},{10,11... | collective-permute-start | bytes 10027016 | tf_op jit(solution)/shard_map/ppermute | solution.py:438
  134.2 14.3 %collective-permute-start.19 = (bf16[192,512]{1,0:T(8,128)(2,1)S(1)}, bf16[192,512]{1,0:T(8,128)(2,1)S(1)}, u32[]{:S(2)}, u32[]{:S(2)}) collective-permute-start(bf16[192,512]{1,0:T(8,128)(2,1)S(1)} %get-tuple-element.98), channel_id=1, source_target_pairs={{0,0},{1,16},{2,2},{3,18},{4,4},{5,20},{6,6},{7,22},{8,8},{9,24},{... | collective-permute-start | bytes 589832 | tf_op jit(solution)/shard_map/ppermute | solution.py:452
  138.3 10.8 %collective-permute-start.20 = (bf16[192,512]{1,0:T(8,128)(2,1)S(1)}, bf16[192,512]{1,0:T(8,128)(2,1)S(1)}, u32[]{:S(2)}, u32[]{:S(2)}) collective-permute-start(bf16[192,512]{1,0:T(8,128)(2,1)S(1)} %get-tuple-element.99), channel_id=1, source_target_pairs={{0,8},{1,24},{2,10},{3,26},{4,12},{5,28},{6,14},{7,30},{8,0},{9,16... | collective-permute-start | bytes 589832 | tf_op jit(solution)/shard_map/ppermute | solution.py:452
  140.0 9.8 %collective-permute-start.21 = (bf16[192,512]{1,0:T(8,128)(2,1)S(1)}, bf16[192,512]{1,0:T(8,128)(2,1)S(1)}, u32[]{:S(2)}, u32[]{:S(2)}) collective-permute-start(bf16[192,512]{1,0:T(8,128)(2,1)S(1)} %get-tuple-element.100), channel_id=1, source_target_pairs={{0,1},{1,17},{2,3},{3,19},{4,5},{5,21},{6,7},{7,23},{8,9},{9,25},{... | collective-permute-start | bytes 589832 | tf_op jit(solution)/shard_map/ppermute | solution.py:452
  150.5 9.5 %collective-permute-start.23 = (bf16[4,1088,384]{2,1,0:T(8,128)(2,1)}, bf16[4,1088,384]{2,1,0:T(8,128)(2,1)}, u32[]{:S(2)}, u32[]{:S(2)}) collective-permute-start(bf16[4,1088,384]{2,1,0:T(8,128)(2,1)} %get-tuple-element.108), channel_id=1, source_target_pairs={{0,1},{1,0},{2,3},{3,2},{4,5},{5,4},{6,7},{7,6},{8,9},{9,8},{10,11... | collective-permute-start | bytes 10027016 | tf_op jit(solution)/shard_map/ppermute | solution.py:438
  154.1 8.8 %collective-permute-start.22 = (bf16[192,512]{1,0:T(8,128)(2,1)}, bf16[192,512]{1,0:T(8,128)(2,1)}, u32[]{:S(2)}, u32[]{:S(2)}) collective-permute-start(bf16[192,512]{1,0:T(8,128)(2,1)} %get-tuple-element.101), channel_id=1, source_target_pairs={{0,9},{1,25},{2,11},{3,27},{4,13},{5,29},{6,15},{7,31},{8,1},{9,17... | collective-permute-start | bytes 589832 | tf_op jit(solution)/shard_map/ppermute | solution.py:452
  162.5 24.6 %collective-permute-start.28 = (bf16[4,544,384]{2,1,0:T(8,128)(2,1)S(1)}, bf16[4,544,384]{2,1,0:T(8,128)(2,1)S(1)}, u32[]{:S(2)}, u32[]{:S(2)}) collective-permute-start(bf16[4,544,384]{2,1,0:T(8,128)(2,1)S(1)} %add_convert_fusion.1), channel_id=1, source_target_pairs={{0,4},{1,3},{2,6},{3,1},{4,0},{5,7},{6,2},{7,5},{8,12},{9,11},{10,... | collective-permute-start | bytes 5013512 | tf_op jit(solution)/shard_map/ppermute | solution.py:504
  166.6 20.5 %copy-start.3 = (bf16[4,1088,384]{2,1,0:T(8,128)(2,1)S(1)}, bf16[4,1088,384]{2,1,0:T(8,128)(2,1)}, u32[]{:S(2)}) copy-start(bf16[4,1088,384]{2,1,0:T(8,128)(2,1)} %copy-done.2) | copy-start | bytes 10027012
  180.2 27.9 %collective-permute-start.24 = (bf16[192,512]{1,0:T(8,128)(2,1)S(1)}, bf16[192,512]{1,0:T(8,128)(2,1)S(1)}, u32[]{:S(2)}, u32[]{:S(2)}) collective-permute-start(bf16[192,512]{1,0:T(8,128)(2,1)S(1)} %get-tuple-element.172), channel_id=1, source_target_pairs={{0,0},{1,16},{2,2},{3,18},{4,4},{5,20},{6,6},{7,22},{8,8},{9,24},{... | collective-permute-start | bytes 589832 | tf_op jit(solution)/shard_map/ppermute | solution.py:452
  183.0 28.6 %collective-permute-start.25 = (bf16[192,512]{1,0:T(8,128)(2,1)S(1)}, bf16[192,512]{1,0:T(8,128)(2,1)S(1)}, u32[]{:S(2)}, u32[]{:S(2)}) collective-permute-start(bf16[192,512]{1,0:T(8,128)(2,1)S(1)} %get-tuple-element.171), channel_id=1, source_target_pairs={{0,8},{1,24},{2,10},{3,26},{4,12},{5,28},{6,14},{7,30},{8,0},{9,16... | collective-permute-start | bytes 589832 | tf_op jit(solution)/shard_map/ppermute | solution.py:452
  184.9 27.5 %collective-permute-start.26 = (bf16[192,512]{1,0:T(8,128)(2,1)S(1)}, bf16[192,512]{1,0:T(8,128)(2,1)S(1)}, u32[]{:S(2)}, u32[]{:S(2)}) collective-permute-start(bf16[192,512]{1,0:T(8,128)(2,1)S(1)} %get-tuple-element.170), channel_id=1, source_target_pairs={{0,16},{1,0},{2,18},{3,2},{4,20},{5,4},{6,22},{7,6},{8,24},{9,8},{... | collective-permute-start | bytes 589832 | tf_op jit(solution)/shard_map/ppermute | solution.py:452
  184.9 27.5 %collective-permute-start.27 = (bf16[192,512]{1,0:T(8,128)(2,1)S(1)}, bf16[192,512]{1,0:T(8,128)(2,1)S(1)}, u32[]{:S(2)}, u32[]{:S(2)}) collective-permute-start(bf16[192,512]{1,0:T(8,128)(2,1)S(1)} %get-tuple-element.169), channel_id=1, source_target_pairs={{0,24},{1,8},{2,26},{3,10},{4,28},{5,12},{6,30},{7,14},{8,16},{9,0... | collective-permute-start | bytes 589832 | tf_op jit(solution)/shard_map/ppermute | solution.py:452
  189.5 15.5 %collective-permute-start.33 = (bf16[4,272,384]{2,1,0:T(8,128)(2,1)S(1)}, bf16[4,272,384]{2,1,0:T(8,128)(2,1)S(1)}, u32[]{:S(2)}, u32[]{:S(2)}) collective-permute-start(bf16[4,272,384]{2,1,0:T(8,128)(2,1)S(1)} %constant_dynamic-slice_fusion.9), channel_id=1, source_target_pairs={{0,2},{1,5},{2,0},{3,7},{4,6},{5,1},{6,4},{7,3},{8,10},{9,13},{10,... | collective-permute-start | bytes 2506760 | tf_op jit(solution)/shard_map/ppermute | solution.py:504
  204.9 21.9 %collective-permute-start.29 = (bf16[192,512]{1,0:T(8,128)(2,1)S(1)}, bf16[192,512]{1,0:T(8,128)(2,1)S(1)}, u32[]{:S(2)}, u32[]{:S(2)}) collective-permute-start(bf16[192,512]{1,0:T(8,128)(2,1)S(1)} %get-tuple-element.168), channel_id=1, source_target_pairs={{0,0},{1,16},{2,2},{3,18},{4,4},{5,20},{6,6},{7,22},{8,8},{9,24},{... | collective-permute-start | bytes 589832 | tf_op jit(solution)/shard_map/ppermute | solution.py:452
  208.8 18.1 %collective-permute-start.30 = (bf16[192,512]{1,0:T(8,128)(2,1)S(1)}, bf16[192,512]{1,0:T(8,128)(2,1)S(1)}, u32[]{:S(2)}, u32[]{:S(2)}) collective-permute-start(bf16[192,512]{1,0:T(8,128)(2,1)S(1)} %get-tuple-element.167), channel_id=1, source_target_pairs={{0,8},{1,24},{2,10},{3,26},{4,12},{5,28},{6,14},{7,30},{8,0},{9,16... | collective-permute-start | bytes 589832 | tf_op jit(solution)/shard_map/ppermute | solution.py:452
  212.3 13.5 %collective-permute-start.38 = (bf16[2,272,384]{2,1,0:T(8,128)(2,1)S(1)}, bf16[2,272,384]{2,1,0:T(8,128)(2,1)S(1)}, u32[]{:S(2)}, u32[]{:S(2)}) collective-permute-start(bf16[2,272,384]{2,1,0:T(8,128)(2,1)S(1)} %pad_maximum_fusion.11), channel_id=1, source_target_pairs={{0,8},{8,0},{16,24},{24,16},{1,9},{9,1},{17,25},{25,17},{2,10},{10... | collective-permute-start | bytes 1253384 | tf_op jit(solution)/shard_map/ppermute | solution.py:438
  212.3 13.5 %copy-start.17 = (bf16[192,512]{1,0:T(8,128)(2,1)}, bf16[192,512]{1,0:T(8,128)(2,1)S(1)}, u32[]{:S(2)}) copy-start(bf16[192,512]{1,0:T(8,128)(2,1)S(1)} %collective-permute-done.26.refs_2_) | copy-start | bytes 589828
  212.3 13.5 %copy-start.19 = (bf16[192,512]{1,0:T(8,128)(2,1)}, bf16[192,512]{1,0:T(8,128)(2,1)S(1)}, u32[]{:S(2)}) copy-start(bf16[192,512]{1,0:T(8,128)(2,1)S(1)} %collective-permute-done.27.refs_3_) | copy-start | bytes 589828
  228.6 7.4 %collective-permute-start.39 = (bf16[1,288,768]{2,1,0:T(8,128)(2,1)}, bf16[1,288,768]{2,1,0:T(8,128)(2,1)S(1)}, u32[]{:S(2)}, u32[]{:S(2)}) collective-permute-start(bf16[1,288,768]{2,1,0:T(8,128)(2,1)} %dynamic-slice_bitcast_fusion), channel_id=1, source_target_pairs={{0,4},{1,3},{2,6},{3,1},{4,0},{5,7},{6,2},{7,5},{8,12},{9,11},{10,... | collective-permute-start | bytes 1327112 | tf_op jit(solution)/shard_map/ppermute | solution.py:504
  228.9 7.7 %collective-permute-start.31 = (bf16[192,512]{1,0:T(8,128)(2,1)}, bf16[192,512]{1,0:T(8,128)(2,1)S(1)}, u32[]{:S(2)}, u32[]{:S(2)}) collective-permute-start(bf16[192,512]{1,0:T(8,128)(2,1)} %get-tuple-element.166), channel_id=1, source_target_pairs={{0,16},{1,0},{2,18},{3,2},{4,20},{5,4},{6,22},{7,6},{8,24},{9,8},{... | collective-permute-start | bytes 589832 | tf_op jit(solution)/shard_map/ppermute | solution.py:452
  231.0 10.0 %collective-permute-start.34 = (bf16[192,512]{1,0:T(8,128)(2,1)S(1)}, bf16[192,512]{1,0:T(8,128)(2,1)S(1)}, u32[]{:S(2)}, u32[]{:S(2)}) collective-permute-start(bf16[192,512]{1,0:T(8,128)(2,1)S(1)} %get-tuple-element.164), channel_id=1, source_target_pairs={{0,0},{1,16},{2,2},{3,18},{4,4},{5,20},{6,6},{7,22},{8,8},{9,24},{... | collective-permute-start | bytes 589832 | tf_op jit(solution)/shard_map/ppermute | solution.py:452
  241.7 6.3 %collective-permute-start.40 = (bf16[1,144,768]{2,1,0:T(8,128)(2,1)}, bf16[1,144,768]{2,1,0:T(8,128)(2,1)}, u32[]{:S(2)}, u32[]{:S(2)}) collective-permute-start(bf16[1,144,768]{2,1,0:T(8,128)(2,1)} %constant_dynamic-slice_fusion.4), channel_id=1, source_target_pairs={{0,2},{1,5},{2,0},{3,7},{4,6},{5,1},{6,4},{7,3},{8,10},{9,13},{10,... | collective-permute-start | bytes 663560 | tf_op jit(solution)/shard_map/ppermute | solution.py:504
  242.8 8.6 %collective-permute-start.32 = (bf16[192,512]{1,0:T(8,128)(2,1)}, bf16[192,512]{1,0:T(8,128)(2,1)S(1)}, u32[]{:S(2)}, u32[]{:S(2)}) collective-permute-start(bf16[192,512]{1,0:T(8,128)(2,1)} %get-tuple-element.165), channel_id=1, source_target_pairs={{0,24},{1,8},{2,26},{3,10},{4,28},{5,12},{6,30},{7,14},{8,16},{9,0... | collective-permute-start | bytes 589832 | tf_op jit(solution)/shard_map/ppermute | solution.py:452
  242.8 13.0 %collective-permute-start.35 = (bf16[192,512]{1,0:T(8,128)(2,1)}, bf16[192,512]{1,0:T(8,128)(2,1)S(1)}, u32[]{:S(2)}, u32[]{:S(2)}) collective-permute-start(bf16[192,512]{1,0:T(8,128)(2,1)} %get-tuple-element.163), channel_id=1, source_target_pairs={{0,8},{1,24},{2,10},{3,26},{4,12},{5,28},{6,14},{7,30},{8,0},{9,16... | collective-permute-start | bytes 589832 | tf_op jit(solution)/shard_map/ppermute | solution.py:452
  247.6 16.3 %collective-permute-start.44 = (bf16[272,384]{1,0:T(8,128)(2,1)}, bf16[272,384]{1,0:T(8,128)(2,1)}, u32[]{:S(2)}, u32[]{:S(2)}) collective-permute-start(bf16[272,384]{1,0:T(8,128)(2,1)} %dynamic-slice_bitcast_fusion.1), channel_id=1, source_target_pairs={{0,16},{8,24},{16,0},{24,8},{1,17},{9,25},{17,1},{25,9},{2,18},{10... | collective-permute-start | bytes 626696 | tf_op jit(solution)/shard_map/ppermute | solution.py:438
  257.7 13.5 %copy-start.51 = (bf16[192,512]{1,0:T(8,128)(2,1)S(1)}, bf16[192,512]{1,0:T(8,128)(2,1)}, u32[]{:S(2)}) copy-start(bf16[192,512]{1,0:T(8,128)(2,1)} %get-tuple-element.161) | copy-start | bytes 589828
  260.1 4.8 %collective-permute-start.41 = (bf16[144,192]{1,0:T(8,128)(2,1)S(1)}, bf16[144,192]{1,0:T(8,128)(2,1)S(1)}, u32[]{:S(2)}, u32[]{:S(2)}) collective-permute-start(bf16[144,192]{1,0:T(8,128)(2,1)S(1)} %bitcast.88), channel_id=1, source_target_pairs={{0,16},{8,24},{16,0},{24,8},{1,17},{9,25},{17,1},{25,9},{2,18},{10... | collective-permute-start | bytes 165896 | tf_op jit(solution)/shard_map/ppermute | solution.py:438
  260.2 4.7 %collective-permute-start.42 = (bf16[144,192]{1,0:T(8,128)(2,1)S(1)}, bf16[144,192]{1,0:T(8,128)(2,1)S(1)}, u32[]{:S(2)}, u32[]{:S(2)}) collective-permute-start(bf16[144,192]{1,0:T(8,128)(2,1)S(1)} %bitcast.89), channel_id=1, source_target_pairs={{0,8},{8,0},{16,24},{24,16},{1,9},{9,1},{17,25},{25,17},{2,10},{10... | collective-permute-start | bytes 165896 | tf_op jit(solution)/shard_map/ppermute | solution.py:438
  260.2 6.7 %collective-permute-start.43 = (bf16[144,192]{1,0:T(8,128)(2,1)S(1)}, bf16[144,192]{1,0:T(8,128)(2,1)S(1)}, u32[]{:S(2)}, u32[]{:S(2)}) collective-permute-start(bf16[144,192]{1,0:T(8,128)(2,1)S(1)} %bitcast.90), channel_id=1, source_target_pairs={{0,24},{8,16},{16,8},{24,0},{1,25},{9,17},{17,9},{25,1},{2,26},{10... | collective-permute-start | bytes 165896 | tf_op jit(solution)/shard_map/ppermute | solution.py:438
  267.0 13.0 %copy-start.32 = (f32[512,768]{1,0:T(8,128)S(1)}, f32[512,768]{1,0:T(8,128)}, u32[]{:S(2)}) copy-start(f32[512,768]{1,0:T(8,128)} %copy-done.31) | copy-start | bytes 4718596
  267.0 12.9 %copy-start.7 = (bf16[1,512,768]{2,1,0:T(8,128)(2,1)S(1)}, bf16[1,512,768]{2,1,0:T(8,128)(2,1)}, u32[]{:S(2)}) copy-start(bf16[1,512,768]{2,1,0:T(8,128)(2,1)} %param.8) | copy-start | bytes 2359300
  267.0 12.9 %copy-start.14 = (bf16[192,512]{1,0:T(8,128)(2,1)S(1)}, bf16[192,512]{1,0:T(8,128)(2,1)}, u32[]{:S(2)}) copy-start(bf16[192,512]{1,0:T(8,128)(2,1)} %copy-done.13) | copy-start | bytes 589828
  267.0 12.9 %copy-start.16 = (bf16[192,512]{1,0:T(8,128)(2,1)S(1)}, bf16[192,512]{1,0:T(8,128)(2,1)}, u32[]{:S(2)}) copy-start(bf16[192,512]{1,0:T(8,128)(2,1)} %copy-done.15) | copy-start | bytes 589828
  267.1 12.9 %copy-start.18 = (bf16[192,512]{1,0:T(8,128)(2,1)S(1)}, bf16[192,512]{1,0:T(8,128)(2,1)}, u32[]{:S(2)}) copy-start(bf16[192,512]{1,0:T(8,128)(2,1)} %copy-done.17) | copy-start | bytes 589828
  267.1 12.9 %copy-start.20 = (bf16[192,512]{1,0:T(8,128)(2,1)S(1)}, bf16[192,512]{1,0:T(8,128)(2,1)}, u32[]{:S(2)}) copy-start(bf16[192,512]{1,0:T(8,128)(2,1)} %copy-done.19) | copy-start | bytes 589828
  267.1 12.9 %copy-start.22 = (bf16[192,512]{1,0:T(8,128)(2,1)S(1)}, bf16[192,512]{1,0:T(8,128)(2,1)}, u32[]{:S(2)}) copy-start(bf16[192,512]{1,0:T(8,128)(2,1)} %copy-done.21) | copy-start | bytes 589828
  267.1 12.9 %copy-start.24 = (bf16[192,512]{1,0:T(8,128)(2,1)S(1)}, bf16[192,512]{1,0:T(8,128)(2,1)}, u32[]{:S(2)}) copy-start(bf16[192,512]{1,0:T(8,128)(2,1)} %copy-done.23) | copy-start | bytes 589828
  267.2 7.4 %collective-permute-start.45 = (bf16[1,416,384]{2,1,0:T(8,128)(2,1)S(1)}, bf16[1,416,384]{2,1,0:T(8,128)(2,1)S(1)}, u32[]{:S(2)}, u32[]{:S(2)}) collective-permute-start(bf16[1,416,384]{2,1,0:T(8,128)(2,1)S(1)} %maximum_bitcast_fusion), channel_id=1, source_target_pairs={{0,2},{1,5},{2,0},{3,7},{4,6},{5,1},{6,4},{7,3},{8,10},{9,13},{10,... | collective-permute-start | bytes 958472 | tf_op jit(solution)/shard_map/ppermute | solution.py:504
  267.6 7.6 %collective-permute-start.36 = (bf16[192,512]{1,0:T(8,128)(2,1)S(1)}, bf16[192,512]{1,0:T(8,128)(2,1)S(1)}, u32[]{:S(2)}, u32[]{:S(2)}) collective-permute-start(bf16[192,512]{1,0:T(8,128)(2,1)S(1)} %copy-done.52), channel_id=1, source_target_pairs={{0,16},{1,0},{2,18},{3,2},{4,20},{5,4},{6,22},{7,6},{8,24},{9,8},{... | collective-permute-start | bytes 589832 | tf_op jit(solution)/shard_map/ppermute | solution.py:452
  271.2 8.4 %collective-permute-start.37 = (bf16[192,512]{1,0:T(8,128)(2,1)S(1)}, bf16[192,512]{1,0:T(8,128)(2,1)S(1)}, u32[]{:S(2)}, u32[]{:S(2)}) collective-permute-start(bf16[192,512]{1,0:T(8,128)(2,1)S(1)} %copy-done.51), channel_id=1, source_target_pairs={{0,24},{1,8},{2,26},{3,10},{4,28},{5,12},{6,30},{7,14},{8,16},{9,0... | collective-permute-start | bytes 589832 | tf_op jit(solution)/shard_map/ppermute | solution.py:452
  279.5 9.6 %collective-permute-start.46 = (bf16[2,416,384]{2,1,0:T(8,128)(2,1)S(1)}, bf16[2,416,384]{2,1,0:T(8,128)(2,1)S(1)}, u32[]{:S(2)}, u32[]{:S(2)}) collective-permute-start(bf16[2,416,384]{2,1,0:T(8,128)(2,1)S(1)} %pad_maximum_fusion.7), channel_id=1, source_target_pairs={{0,4},{1,3},{2,6},{3,1},{4,0},{5,7},{6,2},{7,5},{8,12},{9,11},{10,... | collective-permute-start | bytes 1916936 | tf_op jit(solution)/shard_map/ppermute | solution.py:504
  289.4 3.7 %collective-permute-start.47 = (bf16[4,416,384]{2,1,0:T(8,128)(2,1)S(1)}, bf16[4,416,384]{2,1,0:T(8,128)(2,1)S(1)}, u32[]{:S(2)}, u32[]{:S(2)}) collective-permute-start(bf16[4,416,384]{2,1,0:T(8,128)(2,1)S(1)} %pad_maximum_fusion.4.mine_ref), channel_id=1, source_target_pairs={{0,1},{1,0},{2,3},{3,2},{4,5},{5,4},{6,7},{7,6},{8,9},{9,8},{10,11... | collective-permute-start | bytes 3833864 | tf_op jit(solution)/shard_map/ppermute | solution.py:438
  (39 other events, 127.1 us)
where the time goes:
time: 303 us; the launch traced here: 297 us
  Pallas kernels  98.5 us (33%)
  waiting for transfers between devices  78.4 us (26%)
  starting transfers between devices  76.2 us (25%)
  local copies, waits for them, and re-layouts  26 us (9%)
  other arithmetic  16.4 us (5%)
    ppermute x22, starting transfers between devices, column(): return lax.ppermute(values, ('fsdp', 'rep'), full)  47.9 us
    ppermute x22, waiting for transfers between devices, column(): return lax.ppermute(values, ('fsdp', 'rep'), full)  43.1 us
    pallas_call x3, Pallas kernels, attend_back(): pl.pallas_call(attend_back_kernel, grid=(count // step,), in_specs=[some,...  40.3 us
    ppermute x16, starting transfers between devices, swap(): return lax.ppermute(values, axis, [(i, i ^ offset) for i in range(size)])  20.5 us
    ppermute x16, waiting for transfers between devices, swap(): return lax.ppermute(values, axis, [(i, i ^ offset) for i in range(size)])  18.8 us
    pallas_call x3, Pallas kernels, attend(): pl.pallas_call(attend_kernel, grid=(count // step,), in_specs=[pl.BlockSp...  18.3 us
    ppermute x10, waiting for transfers between devices, stage_swap(): lax.ppermute(values, 'rep', [(i, i ^ stage_bit(i & 1, ranks, stage)) for...  16.4 us
    unnamed x128, local copies, waits for them, and re-layouts  13.7 us
  transfers between devices with their start and end apart: 48, of which 21 were waited for; matrix products, arithmetic and copies ran while one was open for 8% of the time, Pallas kernels for 27%

commit v1 on v0

--- a/solution.py
+++ b/solution.py
@@ -720,9 +720,9 @@
     into_grad = after(shrink(into_grad[None], r, ranks, stages[-1:]), later[2], last[0])
     into_grad = after(shrink(into_grad, r, ranks, stages[-2::-1]), later[3], last[1])[0]
     grads = add(pick(grads, z >> 1), swap(pick(grads, z >> 1 ^ 1), "fsdp", size, 2))
-    lines = into_grad.shape[0]
-    blocks = into_grad.reshape(lines, size, part).transpose(1, 0, 2)
-    blocks = exchange([pick(blocks, z ^ d) for d in range(size)], size)
+    blocks = exchange(
+        [lax.dynamic_slice_in_dim(into_grad, (z ^ d) * part, part, 1) for d in range(size)], size
+    )
     even, odd = (blocks[0].astype(F32) + blocks[2].astype(F32)), (blocks[1].astype(F32) + blocks[3].astype(F32))
     low = z & 1 == 0
     flat = jnp.concatenate([jnp.where(low, even, odd), jnp.where(low, odd, even)], axis=1).astype(BF16)

time: 303 us -> 302 us (level)
  waiting for transfers between devices: 78.4 us -> 85.8 us
  local copies, waits for them, and re-layouts: 26 us -> 21 us
    ppermute x16, waiting for transfers between devices: 18.8 us -> 23.9 us  [swap(): return lax.ppermute(values, axis, [(i, i ^ offset) for i in range(size)])]
    another operation x2 -> x0, local copies, waits for them, and re-layouts: 4.25 us -> none
    ppermute x22, starting transfers between devices: 47.9 us -> 44.8 us  [column(): return lax.ppermute(values, ('fsdp', 'rep'), full)]
    unnamed x128 -> x123, local copies, waits for them, and re-layouts: 13.7 us -> 14.3 us
  transfers between devices with their start and end apart: 48 -> 48, of which waited for: 21 -> 22; matrix products, arithmetic and copies ran while one was open for 8% -> 7% of each run, Pallas kernels for 27% -> 27%
where the time goes in v1:
time: 302 us; the launch traced here: 297 us
  Pallas kernels  98.6 us (33%)
  waiting for transfers between devices  85.8 us (28%)
  starting transfers between devices  73.6 us (24%)
  local copies, waits for them, and re-layouts  21 us (7%)
  other arithmetic  15.7 us (5%)
    ppermute x22, starting transfers between devices, column(): return lax.ppermute(values, ('fsdp', 'rep'), full)  44.8 us
    ppermute x22, waiting for transfers between devices, column(): return lax.ppermute(values, ('fsdp', 'rep'), full)  44.6 us
    pallas_call x3, Pallas kernels, attend_back(): pl.pallas_call(attend_back_kernel, grid=(count // step,), in_specs=[some,...  40.3 us
    ppermute x16, waiting for transfers between devices, swap(): return lax.ppermute(values, axis, [(i, i ^ offset) for i in range(size)])  23.9 us
    ppermute x16, starting transfers between devices, swap(): return lax.ppermute(values, axis, [(i, i ^ offset) for i in range(size)])  20.2 us
    pallas_call x3, Pallas kernels, attend(): pl.pallas_call(attend_kernel, grid=(count // step,), in_specs=[pl.BlockSp...  18.3 us
    ppermute x10, waiting for transfers between devices, stage_swap(): lax.ppermute(values, 'rep', [(i, i ^ stage_bit(i & 1, ranks, stage)) for...  17.4 us
    unnamed x123, local copies, waits for them, and re-layouts  14.3 us
  transfers between devices with their start and end apart: 48, of which 22 were waited for; matrix products, arithmetic and copies ran while one was open for 7% of the time, Pallas kernels for 27%

profile of v1, /device:TPU:1, one launch (start us, length us, event | category | flops | bytes accessed | tf_op | source)
XLA Modules:
  0.0 296.6 jit_solution(203285086235047212)
XLA Ops:
  0.7 1.3 fusion.11
  2.2 2.2 collective-permute-start.2
  4.4 2.3 collective-permute-start.3
  6.7 2.7 collective-permute-start
  9.5 5.2 %collective-permute-done.4 = bf16[80,768]{1,0:T(8,128)(2,1)S(1)} collective-permute-done((bf16[80,768]{1,0:T(8,128)(2,1)S(1)}, bf16[80,768]{1,0:T(8,128)(2,1)S(1)}, u32[]{:S(2)}, u32[]{:S(2)}) %collective-permute-start.4) | collective-permute-done | bytes 122912 | tf_op jit(solution)/shard_map/ppermute | solution.py:438
  14.7 1.3 collective-permute-start.6
  16.0 6.2 %collective-permute-done.6 = bf16[4,72,768]{2,1,0:T(8,128)(2,1)S(1)} collective-permute-done((bf16[4,72,768]{2,1,0:T(8,128)(2,1)S(1)}, bf16[4,72,768]{2,1,0:T(8,128)(2,1)S(1)}, u32[]{:S(2)}, u32[]{:S(2)}) %collective-permute-start.6) | collective-permute-done | bytes 442400 | tf_op jit(solution)/shard_map/ppermute | solution.py:504
  22.4 12.7 %collective-permute-done = bf16[512,768]{1,0:T(8,128)(2,1)S(1)} collective-permute-done((bf16[512,768]{1,0:T(8,128)(2,1)S(1)}, bf16[512,768]{1,0:T(8,128)(2,1)S(1)}, u32[]{:S(2)}, u32[]{:S(2)}) %collective-permute-start) | collective-permute-done | bytes 786464 | tf_op jit(solution)/shard_map/ppermute | solution.py:452
  38.3 1.9 collective-permute-start.1
  40.5 7.5 %collective-permute-done.7 = bf16[4,144,768]{2,1,0:T(8,128)(2,1)} collective-permute-done((bf16[4,144,768]{2,1,0:T(8,128)(2,1)S(1)}, bf16[4,144,768]{2,1,0:T(8,128)(2,1)}, u32[]{:S(2)}, u32[]{:S(2)}) %collective-permute-start.7) | collective-permute-done | bytes 884768 | tf_op jit(solution)/shard_map/ppermute | solution.py:504
  48.0 1.3 broadcast_select_fusion.3
  49.5 1.8 collective-permute-done.1
  51.3 1.3 broadcast_select_fusion.7
  52.7 1.2 pad_maximum_fusion.3.pair_ref
  55.3 4.6 %collective-permute-start.14 = (bf16[136,768]{1,0:T(8,128)(2,1)S(1)}, bf16[136,768]{1,0:T(8,128)(2,1)S(1)}, u32[]{:S(2)}, u32[]{:S(2)}) collective-permute-start(bf16[136,768]{1,0:T(8,128)(2,1)S(1)} %constant_dynamic-slice_fusion.6), channel_id=1, source_target_pairs={{0,16},{8,24},{16,0},{24,8},{1,17},{9,25},{17,1},{25,9},{2,18},{10... | collective-permute-start | bytes 626696 | tf_op jit(solution)/shard_map/ppermute | solution.py:438
  59.9 10.5 %project.1 = (bf16[2048,768]{1,0:T(8,128)(2,1)S(1)}, bf16[192,2048]{1,0:T(8,128)(2,1)S(1)}, bf16[192,2048]{1,0:T(8,128)(2,1)S(1)}, bf16[192,2048]{1,0:T(8,128)(2,1)S(1)}) custom-call(s32[2]{0:T(128)S(1)} %pad_add_fusion.place_ref, bf16[1024,768]{1,0:T(8,128)(2,1)} %pad_maximum_fusion.3.pair_ref, bf16[1024,768]{1,0:T(8,128)(2,1)} %collective-permute-done.5.other_ref, ...), custom_call_target="tpu_custom_call" | custom-call | flops 8000000000 | bytes 20000000 | tf_op jit(solution)/shard_map/project/pallas_call | solution.py:221
  70.4 1.7 copy-done.33
  72.1 6.1 %attend.3 = (bf16[64,2048]{1,0:T(8,128)(2,1)S(1)}, f32[1,2048]{1,0:T(1,128)S(1)}) custom-call(bf16[192,2048]{1,0:T(8,128)(2,1)S(1)} %get-tuple-element.81.q_ref, bf16[192,2048]{1,0:T(8,128)(2,1)S(1)} %get-tuple-element.87.k_ref.kt_ref, bf16[192,2048]{1,0:T(8,128)(2,1)S(1)} %get-tuple-element.83.v_ref.vt_ref), custom_call_target="tpu_custom_call" | custom-call | flops 7516192768 | bytes 1048576 | tf_op jit(solution)/shard_map/attend/pallas_call | solution.py:43
  78.7 6.1 %attend.4 = (bf16[64,2048]{1,0:T(8,128)(2,1)S(1)}, f32[1,2048]{1,0:T(1,128)S(1)}) custom-call(bf16[192,2048]{1,0:T(8,128)(2,1)S(1)} %get-tuple-element.81.q_ref, bf16[192,2048]{1,0:T(8,128)(2,1)S(1)} %get-tuple-element.87.k_ref.kt_ref, bf16[192,2048]{1,0:T(8,128)(2,1)S(1)} %get-tuple-element.83.v_ref.vt_ref), custom_call_target="tpu_custom_call" | custom-call | flops 7516192768 | bytes 1048576 | tf_op jit(solution)/shard_map/attend/pallas_call | solution.py:43
  84.8 6.1 %attend.5 = (bf16[64,2048]{1,0:T(8,128)(2,1)S(1)}, f32[1,2048]{1,0:T(1,128)S(1)}) custom-call(bf16[192,2048]{1,0:T(8,128)(2,1)S(1)} %get-tuple-element.81.q_ref, bf16[192,2048]{1,0:T(8,128)(2,1)S(1)} %get-tuple-element.87.k_ref.kt_ref, bf16[192,2048]{1,0:T(8,128)(2,1)S(1)} %get-tuple-element.83.v_ref.vt_ref), custom_call_target="tpu_custom_call" | custom-call | flops 7516192768 | bytes 1048576 | tf_op jit(solution)/shard_map/attend/pallas_call | solution.py:43
  91.2 1.3 collective-permute-start.17
  92.7 4.6 %collective-permute-start.10 = (bf16[192,512]{1,0:T(8,128)(2,1)S(1)}, bf16[192,512]{1,0:T(8,128)(2,1)S(1)}, u32[]{:S(2)}, u32[]{:S(2)}) collective-permute-start(bf16[192,512]{1,0:T(8,128)(2,1)S(1)} %get-tuple-element.175), channel_id=1, source_target_pairs={{0,8},{1,24},{2,10},{3,26},{4,12},{5,28},{6,14},{7,30},{8,0},{9,16... | collective-permute-start | bytes 589832 | tf_op jit(solution)/shard_map/ppermute | solution.py:452
  97.9 2.8 collective-permute-start.9
  100.7 2.2 collective-permute-done.10.m1_ref
  102.9 8.2 %collective-permute-done.11.m2_ref = bf16[192,512]{1,0:T(8,128)(2,1)S(1)} collective-permute-done((bf16[192,512]{1,0:T(8,128)(2,1)S(1)}, bf16[192,512]{1,0:T(8,128)(2,1)S(1)}, u32[]{:S(2)}, u32[]{:S(2)}) %collective-permute-start.11) | collective-permute-done | bytes 196640 | tf_op jit(solution)/shard_map/ppermute | solution.py:452
  113.1 2.5 collective-permute-start.18
  115.6 5.6 %collective-permute-done.18.theirs_ref = bf16[4,544,768]{2,1,0:T(8,128)(2,1)S(1)} collective-permute-done((bf16[4,544,768]{2,1,0:T(8,128)(2,1)S(1)}, bf16[4,544,768]{2,1,0:T(8,128)(2,1)S(1)}, u32[]{:S(2)}, u32[]{:S(2)}) %collective-permute-start.18) | collective-permute-done | bytes 3342368 | tf_op jit(solution)/shard_map/ppermute | solution.py:438
  121.2 13.1 %forward_back.1 = (bf16[512,768]{1,0:T(8,128)(2,1)}, f32[512,768]{1,0:T(8,128)S(1)}, bf16[512,768]{1,0:T(8,128)(2,1)S(1)}, bf16[512,768]{1,0:T(8,128)(2,1)S(1)},...) custom-call(s32[2]{0:T(128)S(1)} %pad_add_fusion.place_ref, ...), custom_call_target="tpu_custom_call" | custom-call | flops 14000000000 | bytes 20000000 | tf_op jit(solution)/shard_map/forward_back/pallas_call | solution.py:326
  134.3 4.1 %collective-permute-start.19 = (bf16[192,512]{1,0:T(8,128)(2,1)S(1)}, bf16[192,512]{1,0:T(8,128)(2,1)S(1)}, u32[]{:S(2)}, u32[]{:S(2)}) collective-permute-start(bf16[192,512]{1,0:T(8,128)(2,1)S(1)} %get-tuple-element.98), channel_id=1, source_target_pairs={{0,0},{1,16},{2,2},{3,18},{4,4},{5,20},{6,6},{7,22},{8,8},{9,24},{... | collective-permute-start | bytes 589832 | tf_op jit(solution)/shard_map/ppermute | solution.py:452
  138.4 1.7 collective-permute-start.20
  140.1 5.2 %gradients.1 = (bf16[4,1088,384]{2,1,0:T(8,128)(2,1)S(1)}, bf16[4,1088,384]{2,1,0:T(8,128)(2,1)}) custom-call(s32[2]{0:T(128)S(1)} %pad_add_fusion.place_ref, bf16[192,512]{1,0:T(8,128)(2,1)S(1)} %collective-permute-done.9.m0_ref, bf16[192,512]{1,0:T(8,128)(2,1)S(1)} %collective-permute-done.10.m1_ref, bf16[192,512]{1,0:T(8,128)(2,1)S(1)} %collective-permute-done.11.m2_ref, ...), custom_call_target="tpu_custom_call" | custom-call | flops 12000000000 | bytes 12000000 | tf_op jit(solution)/shard_map/gradients/pallas_call | solution.py:369
  145.3 1.7 copy-done.2
  147.0 1.5 collective-permute-done.19.u0_ref
  150.6 3.5 %collective-permute-start.23 = (bf16[4,1088,384]{2,1,0:T(8,128)(2,1)}, bf16[4,1088,384]{2,1,0:T(8,128)(2,1)}, u32[]{:S(2)}, u32[]{:S(2)}) collective-permute-start(bf16[4,1088,384]{2,1,0:T(8,128)(2,1)} %get-tuple-element.108), channel_id=1, source_target_pairs={{0,1},{1,0},{2,3},{3,2},{4,5},{5,4},{6,7},{7,6},{8,9},{9,8},{10,11... | collective-permute-start | bytes 10027016 | tf_op jit(solution)/shard_map/ppermute | solution.py:438
  154.1 2.6 collective-permute-start.22
  156.7 3.4 %collective-permute-done.23 = bf16[4,1088,384]{2,1,0:T(8,128)(2,1)} collective-permute-done((bf16[4,1088,384]{2,1,0:T(8,128)(2,1)}, bf16[4,1088,384]{2,1,0:T(8,128)(2,1)}, u32[]{:S(2)}, u32[]{:S(2)}) %collective-permute-start.23) | collective-permute-done | bytes 3342368 | tf_op jit(solution)/shard_map/ppermute | solution.py:438
  160.1 2.5 add_convert_fusion.1
  166.7 13.5 %attend_back.3 = (bf16[192,2048]{1,0:T(8,128)(2,1)S(1)}, bf16[192,768]{1,0:T(8,128)(2,1)S(1)}) custom-call(bf16[192,2048]{1,0:T(8,128)(2,1)S(1)} %copy-done.36, bf16[192,2048]{1,0:T(8,128)(2,1)S(1)} %copy-done.39, bf16[192,2048]{1,0:T(8,128)(2,1)S(1)} %copy-done.42, bf16[192,512]{1,0:T(8,128)(2,1)S(1)} %copy-done.26, bf16[192,512]{1,0:T(8,128)(2,1)S(1)} %copy-done.28, ...), custom_call_target="tpu_custom_call" | custom-call | flops 15032385536 | bytes 2097152 | tf_op jit(solution)/shard_map/attend_back/pallas_call | solution.py:113
  180.3 2.8 collective-permute-start.24
  183.1 1.8 collective-permute-start.25
  184.9 2.3 collective-permute-start.27
  187.3 2.2 add_convert_fusion
  190.8 13.3 %attend_back.4 = (bf16[192,2048]{1,0:T(8,128)(2,1)S(1)}, bf16[192,768]{1,0:T(8,128)(2,1)S(1)}) custom-call(bf16[192,2048]{1,0:T(8,128)(2,1)S(1)} %copy-done.37, bf16[192,2048]{1,0:T(8,128)(2,1)S(1)} %copy-done.40, bf16[192,2048]{1,0:T(8,128)(2,1)S(1)} %copy-done.43, bf16[192,512]{1,0:T(8,128)(2,1)S(1)} %copy-done.26, bf16[192,512]{1,0:T(8,128)(2,1)S(1)} %copy-done.28, ...), custom_call_target="tpu_custom_call" | custom-call | flops 15032385536 | bytes 2097152 | tf_op jit(solution)/shard_map/attend_back/pallas_call | solution.py:113
  205.0 2.7 collective-permute-start.29
  208.8 2.8 collective-permute-start.30
  212.3 13.5 %attend_back.5 = (bf16[192,2048]{1,0:T(8,128)(2,1)S(1)}, bf16[192,768]{1,0:T(8,128)(2,1)S(1)}) custom-call(bf16[192,2048]{1,0:T(8,128)(2,1)S(1)} %copy-done.37, bf16[192,2048]{1,0:T(8,128)(2,1)S(1)} %copy-done.40, bf16[192,2048]{1,0:T(8,128)(2,1)S(1)} %copy-done.43, bf16[192,512]{1,0:T(8,128)(2,1)S(1)} %copy-done.26, bf16[192,512]{1,0:T(8,128)(2,1)S(1)} %copy-done.28, ...), custom_call_target="tpu_custom_call" | custom-call | flops 15032385536 | bytes 2097152 | tf_op jit(solution)/shard_map/attend_back/pallas_call | solution.py:113
  228.7 2.1 fusion.12
  230.9 4.3 %collective-permute-start.34 = (bf16[192,512]{1,0:T(8,128)(2,1)S(1)}, bf16[192,512]{1,0:T(8,128)(2,1)S(1)}, u32[]{:S(2)}, u32[]{:S(2)}) collective-permute-start(bf16[192,512]{1,0:T(8,128)(2,1)S(1)} %get-tuple-element.164), channel_id=1, source_target_pairs={{0,0},{1,16},{2,2},{3,18},{4,4},{5,20},{6,6},{7,22},{8,8},{9,24},{... | collective-permute-start | bytes 589832 | tf_op jit(solution)/shard_map/ppermute | solution.py:452
  236.9 4.0 %collective-permute-done.34.refs_8_ = bf16[192,512]{1,0:T(8,128)(2,1)S(1)} collective-permute-done((bf16[192,512]{1,0:T(8,128)(2,1)S(1)}, bf16[192,512]{1,0:T(8,128)(2,1)S(1)}, u32[]{:S(2)}, u32[]{:S(2)}) %collective-permute-start.34) | collective-permute-done | bytes 196640 | tf_op jit(solution)/shard_map/ppermute | solution.py:452
  242.7 3.1 %collective-permute-start.35 = (bf16[192,512]{1,0:T(8,128)(2,1)}, bf16[192,512]{1,0:T(8,128)(2,1)S(1)}, u32[]{:S(2)}, u32[]{:S(2)}) collective-permute-start(bf16[192,512]{1,0:T(8,128)(2,1)} %get-tuple-element.163), channel_id=1, source_target_pairs={{0,8},{1,24},{2,10},{3,26},{4,12},{5,28},{6,14},{7,30},{8,0},{9,16... | collective-permute-start | bytes 589832 | tf_op jit(solution)/shard_map/ppermute | solution.py:452
  248.2 3.0 %collective-permute-done.32.refs_7_ = bf16[192,512]{1,0:T(8,128)(2,1)S(1)} collective-permute-done((bf16[192,512]{1,0:T(8,128)(2,1)}, bf16[192,512]{1,0:T(8,128)(2,1)S(1)}, u32[]{:S(2)}, u32[]{:S(2)}) %collective-permute-start.32) | collective-permute-done | bytes 196640 | tf_op jit(solution)/shard_map/ppermute | solution.py:452
  251.3 4.3 %collective-permute-done.35.refs_9_ = bf16[192,512]{1,0:T(8,128)(2,1)S(1)} collective-permute-done((bf16[192,512]{1,0:T(8,128)(2,1)}, bf16[192,512]{1,0:T(8,128)(2,1)S(1)}, u32[]{:S(2)}, u32[]{:S(2)}) %collective-permute-start.35) | collective-permute-done | bytes 196640 | tf_op jit(solution)/shard_map/ppermute | solution.py:452
  256.0 3.4 %collective-permute-start.43 = (bf16[144,192]{1,0:T(8,128)(2,1)S(1)}, bf16[144,192]{1,0:T(8,128)(2,1)S(1)}, u32[]{:S(2)}, u32[]{:S(2)}) collective-permute-start(bf16[144,192]{1,0:T(8,128)(2,1)S(1)} %get-tuple-element.184), channel_id=1, source_target_pairs={{0,24},{8,16},{16,8},{24,0},{1,25},{9,17},{17,9},{25,1},{2,26},{10... | collective-permute-start | bytes 165896 | tf_op jit(solution)/shard_map/ppermute | solution.py:438
  259.3 4.8 %collective-permute-done.44 = bf16[272,384]{1,0:T(8,128)(2,1)S(1)} collective-permute-done((bf16[272,384]{1,0:T(8,128)(2,1)S(1)}, bf16[272,384]{1,0:T(8,128)(2,1)S(1)}, u32[]{:S(2)}, u32[]{:S(2)}) %collective-permute-start.44) | collective-permute-done | bytes 208928 | tf_op jit(solution)/shard_map/ppermute | solution.py:438
  264.3 2.3 collective-permute-done.41
  267.7 1.5 collective-permute-start.36
  269.2 2.3 collective-permute-start.37
  271.6 1.5 collective-permute-done.45
  273.3 2.2 collective-permute-done.36.refs_10_
  275.5 3.5 %collective-permute-done.37.refs_11_ = bf16[192,512]{1,0:T(8,128)(2,1)S(1)} collective-permute-done((bf16[192,512]{1,0:T(8,128)(2,1)S(1)}, bf16[192,512]{1,0:T(8,128)(2,1)S(1)}, u32[]{:S(2)}, u32[]{:S(2)}) %collective-permute-start.37) | collective-permute-done | bytes 196640 | tf_op jit(solution)/shard_map/ppermute | solution.py:452
  279.9 7.0 %token_back.1 = f32[512,768]{1,0:T(8,128)} custom-call(s32[2]{0:T(128)S(1)} %pad_add_fusion.place_ref, bf16[192,512]{1,0:T(8,128)(2,1)S(1)} %copy-done.14, bf16[192,512]{1,0:T(8,128)(2,1)S(1)} %copy-done.16, bf16[192,512]{1,0:T(8,128)(2,1)S(1)} %copy-done.18, bf16[192,512]{1,0:T(8,128)(2,1)S(1)} %copy-done.20, bf16[192,512]{1,0:T(8,128)(2,1)S(1)} %copy-done.22, ...), custom_call_target="tpu_custom_call" | custom-call | flops 5000000000 | bytes 12000000 | tf_op jit(solution)/shard_map/token_back/pallas_call | solution.py:414
  287.0 1.6 collective-permute-done.46
  289.6 2.6 collective-permute-done.47.other_ref
  292.2 4.2 %finish.1 = (f32[192,2304]{1,0:T(8,128)}, f32[1,192]{1,0:T(1,128)}, f32[192,768]{1,0:T(8,128)}, f32[192,2304]{1,0:T(8,128)}, f32[1,192]{1,0:T(1,128)}, /*index=5*/f32[288,768]{1,0:T(8,128)}) custom-call(s32[2]{0:T(128)S(1)} %pad_add_fusion.place_ref, bf16[4,416,384]{2,1,0:T(8,128)(2,1)S(1)} %pad_maximum_fusion.4.mine_ref, ...), custom_call_target="tpu_custom_call" | custom-call | tf_op jit(solution)/shard_map/finish/pallas_call | solution.py:614
  (225 shorter events, 31.5 us)
Async XLA Ops:
  2.2 7.3 %collective-permute-start.2 = (bf16[80,768]{1,0:T(8,128)(2,1)S(1)}, bf16[80,768]{1,0:T(8,128)(2,1)S(1)}, u32[]{:S(2)}, u32[]{:S(2)}) collective-permute-start(bf16[80,768]{1,0:T(8,128)(2,1)S(1)} %get-tuple-element.187), channel_id=1, source_target_pairs={{0,8},{8,0},{16,24},{24,16},{1,9},{9,1},{17,25},{25,17},{2,10},{10... | collective-permute-start | bytes 368648 | tf_op jit(solution)/shard_map/ppermute | solution.py:438
  4.4 5.1 %collective-permute-start.3 = (bf16[80,768]{1,0:T(8,128)(2,1)S(1)}, bf16[80,768]{1,0:T(8,128)(2,1)S(1)}, u32[]{:S(2)}, u32[]{:S(2)}) collective-permute-start(bf16[80,768]{1,0:T(8,128)(2,1)S(1)} %get-tuple-element.187), channel_id=1, source_target_pairs={{0,16},{8,24},{16,0},{24,8},{1,17},{9,25},{17,1},{25,9},{2,18},{10... | collective-permute-start | bytes 368648 | tf_op jit(solution)/shard_map/ppermute | solution.py:438
  6.7 7.9 %collective-permute-start.4 = (bf16[80,768]{1,0:T(8,128)(2,1)S(1)}, bf16[80,768]{1,0:T(8,128)(2,1)S(1)}, u32[]{:S(2)}, u32[]{:S(2)}) collective-permute-start(bf16[80,768]{1,0:T(8,128)(2,1)S(1)} %get-tuple-element.187), channel_id=1, source_target_pairs={{0,24},{8,16},{16,8},{24,0},{1,25},{9,17},{17,9},{25,1},{2,26},{10... | collective-permute-start | bytes 368648 | tf_op jit(solution)/shard_map/ppermute | solution.py:438
  6.7 28.4 %collective-permute-start = (bf16[512,768]{1,0:T(8,128)(2,1)S(1)}, bf16[512,768]{1,0:T(8,128)(2,1)S(1)}, u32[]{:S(2)}, u32[]{:S(2)}) collective-permute-start(bf16[512,768]{1,0:T(8,128)(2,1)S(1)} %bitcast.57), channel_id=1, source_target_pairs={{0,8},{1,16},{2,10},{3,18},{4,12},{5,20},{6,14},{7,22},{8,0},{9,24... | collective-permute-start | bytes 2359304 | tf_op jit(solution)/shard_map/ppermute | solution.py:452
  14.7 7.5 %collective-permute-start.6 = (bf16[4,72,768]{2,1,0:T(8,128)(2,1)S(1)}, bf16[4,72,768]{2,1,0:T(8,128)(2,1)S(1)}, u32[]{:S(2)}, u32[]{:S(2)}) collective-permute-start(bf16[4,72,768]{2,1,0:T(8,128)(2,1)S(1)} %pad_maximum_fusion.8), channel_id=1, source_target_pairs={{0,2},{1,5},{2,0},{3,7},{4,6},{5,1},{6,4},{7,3},{8,10},{9,13},{10,... | collective-permute-start | bytes 1327112 | tf_op jit(solution)/shard_map/ppermute | solution.py:504
  36.0 12.0 %collective-permute-start.7 = (bf16[4,144,768]{2,1,0:T(8,128)(2,1)S(1)}, bf16[4,144,768]{2,1,0:T(8,128)(2,1)}, u32[]{:S(2)}, u32[]{:S(2)}) collective-permute-start(bf16[4,144,768]{2,1,0:T(8,128)(2,1)S(1)} %pad_maximum_fusion.5), channel_id=1, source_target_pairs={{0,4},{1,3},{2,6},{3,1},{4,0},{5,7},{6,2},{7,5},{8,12},{9,11},{10,... | collective-permute-start | bytes 2654216 | tf_op jit(solution)/shard_map/ppermute | solution.py:504
  38.2 21.7 %copy-start.8 = (f32[32,2048]{1,0:T(8,128)}, f32[32,2048]{1,0:T(8,128)S(1)}, u32[]{:S(2)}) copy-start(f32[32,2048]{1,0:T(8,128)S(1)} %get-tuple-element.79.sin_ref) | copy-start | bytes 786436
  38.2 21.7 %copy-start.10 = (f32[32,2048]{1,0:T(8,128)}, f32[32,2048]{1,0:T(8,128)S(1)}, u32[]{:S(2)}) copy-start(f32[32,2048]{1,0:T(8,128)S(1)} %get-tuple-element.78.cos_ref) | copy-start | bytes 786436
  38.3 13.1 %collective-permute-start.1 = (bf16[512,768]{1,0:T(8,128)(2,1)}, bf16[512,768]{1,0:T(8,128)(2,1)}, u32[]{:S(2)}, u32[]{:S(2)}) collective-permute-start(bf16[512,768]{1,0:T(8,128)(2,1)} %copy-done.47), channel_id=1, source_target_pairs={{1,9},{3,11},{5,13},{7,15},{9,1},{11,3},{13,5},{15,7},{16,24},{18,... | collective-permute-start | bytes 2359304 | tf_op jit(solution)/shard_map/ppermute | solution.py:452
  49.5 10.4 %collective-permute-start.8 = (bf16[4,288,768]{2,1,0:T(8,128)(2,1)S(1)}, bf16[4,288,768]{2,1,0:T(8,128)(2,1)}, u32[]{:S(2)}, u32[]{:S(2)}) collective-permute-start(bf16[4,288,768]{2,1,0:T(8,128)(2,1)S(1)} %pad_maximum_fusion.1.mine_ref.refs_12_), channel_id=1, source_target_pairs={{0,1},{1,0},{2,3},{3,2},{4,5},{5,4},{6,7},{7,6},{8,9},{9,8},{10,11... | collective-permute-start | bytes 5308424 | tf_op jit(solution)/shard_map/ppermute | solution.py:438
  53.9 6.0 %collective-permute-start.5 = (bf16[1024,768]{1,0:T(8,128)(2,1)}, bf16[1024,768]{1,0:T(8,128)(2,1)}, u32[]{:S(2)}, u32[]{:S(2)}) collective-permute-start(bf16[1024,768]{1,0:T(8,128)(2,1)} %pad_maximum_fusion.3.pair_ref), channel_id=1, source_target_pairs={{0,1},{1,0},{2,3},{3,2},{4,5},{5,4},{6,7},{7,6},{8,9},{9,8},{10,11... | collective-permute-start | bytes 4718600 | tf_op jit(solution)/shard_map/ppermute | solution.py:438
  55.2 23.0 %collective-permute-start.13 = (bf16[136,768]{1,0:T(8,128)(2,1)S(1)}, bf16[136,768]{1,0:T(8,128)(2,1)S(1)}, u32[]{:S(2)}, u32[]{:S(2)}) collective-permute-start(bf16[136,768]{1,0:T(8,128)(2,1)S(1)} %constant_dynamic-slice_fusion.6), channel_id=1, source_target_pairs={{0,8},{8,0},{16,24},{24,16},{1,9},{9,1},{17,25},{25,17},{2,10},{10... | collective-permute-start | bytes 626696 | tf_op jit(solution)/shard_map/ppermute | solution.py:438
  55.3 23.0 %collective-permute-start.14 = (bf16[136,768]{1,0:T(8,128)(2,1)S(1)}, bf16[136,768]{1,0:T(8,128)(2,1)S(1)}, u32[]{:S(2)}, u32[]{:S(2)}) collective-permute-start(bf16[136,768]{1,0:T(8,128)(2,1)S(1)} %constant_dynamic-slice_fusion.6), channel_id=1, source_target_pairs={{0,16},{8,24},{16,0},{24,8},{1,17},{9,25},{17,1},{25,9},{2,18},{10... | collective-permute-start | bytes 626696 | tf_op jit(solution)/shard_map/ppermute | solution.py:438
  59.9 18.4 %collective-permute-start.15 = (bf16[136,768]{1,0:T(8,128)(2,1)S(1)}, bf16[136,768]{1,0:T(8,128)(2,1)S(1)}, u32[]{:S(2)}, u32[]{:S(2)}) collective-permute-start(bf16[136,768]{1,0:T(8,128)(2,1)S(1)} %constant_dynamic-slice_fusion.6), channel_id=1, source_target_pairs={{0,24},{8,16},{16,8},{24,0},{1,25},{9,17},{17,9},{25,1},{2,26},{10... | collective-permute-start | bytes 626696 | tf_op jit(solution)/shard_map/ppermute | solution.py:438
  78.4 12.5 %collective-permute-start.16 = (bf16[4,136,768]{2,1,0:T(8,128)(2,1)S(1)}, bf16[4,136,768]{2,1,0:T(8,128)(2,1)S(1)}, u32[]{:S(2)}, u32[]{:S(2)}) collective-permute-start(bf16[4,136,768]{2,1,0:T(8,128)(2,1)S(1)} %pad_maximum_fusion.6), channel_id=1, source_target_pairs={{0,2},{1,5},{2,0},{3,7},{4,6},{5,1},{6,4},{7,3},{8,10},{9,13},{10,... | collective-permute-start | bytes 2506760 | tf_op jit(solution)/shard_map/ppermute | solution.py:504
  91.2 21.0 %collective-permute-start.17 = (bf16[4,272,768]{2,1,0:T(8,128)(2,1)S(1)}, bf16[4,272,768]{2,1,0:T(8,128)(2,1)S(1)}, u32[]{:S(2)}, u32[]{:S(2)}) collective-permute-start(bf16[4,272,768]{2,1,0:T(8,128)(2,1)S(1)} %pad_maximum_fusion.2), channel_id=1, source_target_pairs={{0,4},{1,3},{2,6},{3,1},{4,0},{5,7},{6,2},{7,5},{8,12},{9,11},{10,... | collective-permute-start | bytes 5013512 | tf_op jit(solution)/shard_map/ppermute | solution.py:504
  92.7 10.2 %collective-permute-start.10 = (bf16[192,512]{1,0:T(8,128)(2,1)S(1)}, bf16[192,512]{1,0:T(8,128)(2,1)S(1)}, u32[]{:S(2)}, u32[]{:S(2)}) collective-permute-start(bf16[192,512]{1,0:T(8,128)(2,1)S(1)} %get-tuple-element.175), channel_id=1, source_target_pairs={{0,8},{1,24},{2,10},{3,26},{4,12},{5,28},{6,14},{7,30},{8,0},{9,16... | collective-permute-start | bytes 589832 | tf_op jit(solution)/shard_map/ppermute | solution.py:452
  97.3 13.9 %collective-permute-start.11 = (bf16[192,512]{1,0:T(8,128)(2,1)S(1)}, bf16[192,512]{1,0:T(8,128)(2,1)S(1)}, u32[]{:S(2)}, u32[]{:S(2)}) collective-permute-start(bf16[192,512]{1,0:T(8,128)(2,1)S(1)} %get-tuple-element.174), channel_id=1, source_target_pairs={{0,16},{1,0},{2,18},{3,2},{4,20},{5,4},{6,22},{7,6},{8,24},{9,8},{... | collective-permute-start | bytes 589832 | tf_op jit(solution)/shard_map/ppermute | solution.py:452
  97.3 13.9 %collective-permute-start.12 = (bf16[192,512]{1,0:T(8,128)(2,1)S(1)}, bf16[192,512]{1,0:T(8,128)(2,1)S(1)}, u32[]{:S(2)}, u32[]{:S(2)}) collective-permute-start(bf16[192,512]{1,0:T(8,128)(2,1)S(1)} %get-tuple-element.173), channel_id=1, source_target_pairs={{0,24},{1,8},{2,26},{3,10},{4,28},{5,12},{6,30},{7,14},{8,16},{9,0... | collective-permute-start | bytes 589832 | tf_op jit(solution)/shard_map/ppermute | solution.py:452
  97.9 14.3 %collective-permute-start.9 = (bf16[192,512]{1,0:T(8,128)(2,1)S(1)}, bf16[192,512]{1,0:T(8,128)(2,1)S(1)}, u32[]{:S(2)}, u32[]{:S(2)}) collective-permute-start(bf16[192,512]{1,0:T(8,128)(2,1)S(1)} %get-tuple-element.176), channel_id=1, source_target_pairs={{0,0},{1,16},{2,2},{3,18},{4,4},{5,20},{6,6},{7,22},{8,8},{9,24},{... | collective-permute-start | bytes 589832 | tf_op jit(solution)/shard_map/ppermute | solution.py:452
  113.1 8.0 %collective-permute-start.18 = (bf16[4,544,768]{2,1,0:T(8,128)(2,1)S(1)}, bf16[4,544,768]{2,1,0:T(8,128)(2,1)S(1)}, u32[]{:S(2)}, u32[]{:S(2)}) collective-permute-start(bf16[4,544,768]{2,1,0:T(8,128)(2,1)S(1)} %pad_maximum_fusion.mine_ref), channel_id=1, source_target_pairs={{0,1},{1,0},{2,3},{3,2},{4,5},{5,4},{6,7},{7,6},{8,9},{9,8},{10,11... | collective-permute-start | bytes 10027016 | tf_op jit(solution)/shard_map/ppermute | solution.py:438
  134.3 14.3 %collective-permute-start.19 = (bf16[192,512]{1,0:T(8,128)(2,1)S(1)}, bf16[192,512]{1,0:T(8,128)(2,1)S(1)}, u32[]{:S(2)}, u32[]{:S(2)}) collective-permute-start(bf16[192,512]{1,0:T(8,128)(2,1)S(1)} %get-tuple-element.98), channel_id=1, source_target_pairs={{0,0},{1,16},{2,2},{3,18},{4,4},{5,20},{6,6},{7,22},{8,8},{9,24},{... | collective-permute-start | bytes 589832 | tf_op jit(solution)/shard_map/ppermute | solution.py:452
  138.4 10.8 %collective-permute-start.20 = (bf16[192,512]{1,0:T(8,128)(2,1)S(1)}, bf16[192,512]{1,0:T(8,128)(2,1)S(1)}, u32[]{:S(2)}, u32[]{:S(2)}) collective-permute-start(bf16[192,512]{1,0:T(8,128)(2,1)S(1)} %get-tuple-element.99), channel_id=1, source_target_pairs={{0,8},{1,24},{2,10},{3,26},{4,12},{5,28},{6,14},{7,30},{8,0},{9,16... | collective-permute-start | bytes 589832 | tf_op jit(solution)/shard_map/ppermute | solution.py:452
  140.1 9.8 %collective-permute-start.21 = (bf16[192,512]{1,0:T(8,128)(2,1)S(1)}, bf16[192,512]{1,0:T(8,128)(2,1)S(1)}, u32[]{:S(2)}, u32[]{:S(2)}) collective-permute-start(bf16[192,512]{1,0:T(8,128)(2,1)S(1)} %get-tuple-element.100), channel_id=1, source_target_pairs={{0,1},{1,17},{2,3},{3,19},{4,5},{5,21},{6,7},{7,23},{8,9},{9,25},{... | collective-permute-start | bytes 589832 | tf_op jit(solution)/shard_map/ppermute | solution.py:452
  150.6 9.5 %collective-permute-start.23 = (bf16[4,1088,384]{2,1,0:T(8,128)(2,1)}, bf16[4,1088,384]{2,1,0:T(8,128)(2,1)}, u32[]{:S(2)}, u32[]{:S(2)}) collective-permute-start(bf16[4,1088,384]{2,1,0:T(8,128)(2,1)} %get-tuple-element.108), channel_id=1, source_target_pairs={{0,1},{1,0},{2,3},{3,2},{4,5},{5,4},{6,7},{7,6},{8,9},{9,8},{10,11... | collective-permute-start | bytes 10027016 | tf_op jit(solution)/shard_map/ppermute | solution.py:438
  154.1 8.8 %collective-permute-start.22 = (bf16[192,512]{1,0:T(8,128)(2,1)}, bf16[192,512]{1,0:T(8,128)(2,1)}, u32[]{:S(2)}, u32[]{:S(2)}) collective-permute-start(bf16[192,512]{1,0:T(8,128)(2,1)} %get-tuple-element.101), channel_id=1, source_target_pairs={{0,9},{1,25},{2,11},{3,27},{4,13},{5,29},{6,15},{7,31},{8,1},{9,17... | collective-permute-start | bytes 589832 | tf_op jit(solution)/shard_map/ppermute | solution.py:452
  162.6 24.7 %collective-permute-start.28 = (bf16[4,544,384]{2,1,0:T(8,128)(2,1)S(1)}, bf16[4,544,384]{2,1,0:T(8,128)(2,1)S(1)}, u32[]{:S(2)}, u32[]{:S(2)}) collective-permute-start(bf16[4,544,384]{2,1,0:T(8,128)(2,1)S(1)} %add_convert_fusion.1), channel_id=1, source_target_pairs={{0,4},{1,3},{2,6},{3,1},{4,0},{5,7},{6,2},{7,5},{8,12},{9,11},{10,... | collective-permute-start | bytes 5013512 | tf_op jit(solution)/shard_map/ppermute | solution.py:504
  166.7 20.6 %copy-start.3 = (bf16[4,1088,384]{2,1,0:T(8,128)(2,1)S(1)}, bf16[4,1088,384]{2,1,0:T(8,128)(2,1)}, u32[]{:S(2)}) copy-start(bf16[4,1088,384]{2,1,0:T(8,128)(2,1)} %copy-done.2) | copy-start | bytes 10027012
  180.3 27.9 %collective-permute-start.24 = (bf16[192,512]{1,0:T(8,128)(2,1)S(1)}, bf16[192,512]{1,0:T(8,128)(2,1)S(1)}, u32[]{:S(2)}, u32[]{:S(2)}) collective-permute-start(bf16[192,512]{1,0:T(8,128)(2,1)S(1)} %get-tuple-element.172), channel_id=1, source_target_pairs={{0,0},{1,16},{2,2},{3,18},{4,4},{5,20},{6,6},{7,22},{8,8},{9,24},{... | collective-permute-start | bytes 589832 | tf_op jit(solution)/shard_map/ppermute | solution.py:452
  183.1 28.6 %collective-permute-start.25 = (bf16[192,512]{1,0:T(8,128)(2,1)S(1)}, bf16[192,512]{1,0:T(8,128)(2,1)S(1)}, u32[]{:S(2)}, u32[]{:S(2)}) collective-permute-start(bf16[192,512]{1,0:T(8,128)(2,1)S(1)} %get-tuple-element.171), channel_id=1, source_target_pairs={{0,8},{1,24},{2,10},{3,26},{4,12},{5,28},{6,14},{7,30},{8,0},{9,16... | collective-permute-start | bytes 589832 | tf_op jit(solution)/shard_map/ppermute | solution.py:452
  184.9 27.4 %collective-permute-start.26 = (bf16[192,512]{1,0:T(8,128)(2,1)S(1)}, bf16[192,512]{1,0:T(8,128)(2,1)S(1)}, u32[]{:S(2)}, u32[]{:S(2)}) collective-permute-start(bf16[192,512]{1,0:T(8,128)(2,1)S(1)} %get-tuple-element.170), channel_id=1, source_target_pairs={{0,16},{1,0},{2,18},{3,2},{4,20},{5,4},{6,22},{7,6},{8,24},{9,8},{... | collective-permute-start | bytes 589832 | tf_op jit(solution)/shard_map/ppermute | solution.py:452
  184.9 27.4 %collective-permute-start.27 = (bf16[192,512]{1,0:T(8,128)(2,1)S(1)}, bf16[192,512]{1,0:T(8,128)(2,1)S(1)}, u32[]{:S(2)}, u32[]{:S(2)}) collective-permute-start(bf16[192,512]{1,0:T(8,128)(2,1)S(1)} %get-tuple-element.169), channel_id=1, source_target_pairs={{0,24},{1,8},{2,26},{3,10},{4,28},{5,12},{6,30},{7,14},{8,16},{9,0... | collective-permute-start | bytes 589832 | tf_op jit(solution)/shard_map/ppermute | solution.py:452
  189.5 15.4 %collective-permute-start.33 = (bf16[4,272,384]{2,1,0:T(8,128)(2,1)S(1)}, bf16[4,272,384]{2,1,0:T(8,128)(2,1)S(1)}, u32[]{:S(2)}, u32[]{:S(2)}) collective-permute-start(bf16[4,272,384]{2,1,0:T(8,128)(2,1)S(1)} %constant_dynamic-slice_fusion.5), channel_id=1, source_target_pairs={{0,2},{1,5},{2,0},{3,7},{4,6},{5,1},{6,4},{7,3},{8,10},{9,13},{10,... | collective-permute-start | bytes 2506760 | tf_op jit(solution)/shard_map/ppermute | solution.py:504
  205.0 21.9 %collective-permute-start.29 = (bf16[192,512]{1,0:T(8,128)(2,1)S(1)}, bf16[192,512]{1,0:T(8,128)(2,1)S(1)}, u32[]{:S(2)}, u32[]{:S(2)}) collective-permute-start(bf16[192,512]{1,0:T(8,128)(2,1)S(1)} %get-tuple-element.168), channel_id=1, source_target_pairs={{0,0},{1,16},{2,2},{3,18},{4,4},{5,20},{6,6},{7,22},{8,8},{9,24},{... | collective-permute-start | bytes 589832 | tf_op jit(solution)/shard_map/ppermute | solution.py:452
  208.8 18.0 %collective-permute-start.30 = (bf16[192,512]{1,0:T(8,128)(2,1)S(1)}, bf16[192,512]{1,0:T(8,128)(2,1)S(1)}, u32[]{:S(2)}, u32[]{:S(2)}) collective-permute-start(bf16[192,512]{1,0:T(8,128)(2,1)S(1)} %get-tuple-element.167), channel_id=1, source_target_pairs={{0,8},{1,24},{2,10},{3,26},{4,12},{5,28},{6,14},{7,30},{8,0},{9,16... | collective-permute-start | bytes 589832 | tf_op jit(solution)/shard_map/ppermute | solution.py:452
  212.3 13.5 %collective-permute-start.38 = (bf16[2,272,384]{2,1,0:T(8,128)(2,1)S(1)}, bf16[2,272,384]{2,1,0:T(8,128)(2,1)S(1)}, u32[]{:S(2)}, u32[]{:S(2)}) collective-permute-start(bf16[2,272,384]{2,1,0:T(8,128)(2,1)S(1)} %pad_maximum_fusion.11), channel_id=1, source_target_pairs={{0,8},{8,0},{16,24},{24,16},{1,9},{9,1},{17,25},{25,17},{2,10},{10... | collective-permute-start | bytes 1253384 | tf_op jit(solution)/shard_map/ppermute | solution.py:438
  212.3 13.5 %copy-start.17 = (bf16[192,512]{1,0:T(8,128)(2,1)}, bf16[192,512]{1,0:T(8,128)(2,1)S(1)}, u32[]{:S(2)}) copy-start(bf16[192,512]{1,0:T(8,128)(2,1)S(1)} %collective-permute-done.26.refs_2_) | copy-start | bytes 589828
  212.3 13.5 %copy-start.19 = (bf16[192,512]{1,0:T(8,128)(2,1)}, bf16[192,512]{1,0:T(8,128)(2,1)S(1)}, u32[]{:S(2)}) copy-start(bf16[192,512]{1,0:T(8,128)(2,1)S(1)} %collective-permute-done.27.refs_3_) | copy-start | bytes 589828
  228.4 7.3 %collective-permute-start.39 = (bf16[1,288,768]{2,1,0:T(8,128)(2,1)S(1)}, bf16[1,288,768]{2,1,0:T(8,128)(2,1)}, u32[]{:S(2)}, u32[]{:S(2)}) collective-permute-start(bf16[1,288,768]{2,1,0:T(8,128)(2,1)S(1)} %dynamic-slice_bitcast_fusion), channel_id=1, source_target_pairs={{0,4},{1,3},{2,6},{3,1},{4,0},{5,7},{6,2},{7,5},{8,12},{9,11},{10,... | collective-permute-start | bytes 1327112 | tf_op jit(solution)/shard_map/ppermute | solution.py:504
  228.7 8.1 %collective-permute-start.31 = (bf16[192,512]{1,0:T(8,128)(2,1)}, bf16[192,512]{1,0:T(8,128)(2,1)S(1)}, u32[]{:S(2)}, u32[]{:S(2)}) collective-permute-start(bf16[192,512]{1,0:T(8,128)(2,1)} %get-tuple-element.166), channel_id=1, source_target_pairs={{0,16},{1,0},{2,18},{3,2},{4,20},{5,4},{6,22},{7,6},{8,24},{9,8},{... | collective-permute-start | bytes 589832 | tf_op jit(solution)/shard_map/ppermute | solution.py:452
  230.9 10.0 %collective-permute-start.34 = (bf16[192,512]{1,0:T(8,128)(2,1)S(1)}, bf16[192,512]{1,0:T(8,128)(2,1)S(1)}, u32[]{:S(2)}, u32[]{:S(2)}) collective-permute-start(bf16[192,512]{1,0:T(8,128)(2,1)S(1)} %get-tuple-element.164), channel_id=1, source_target_pairs={{0,0},{1,16},{2,2},{3,18},{4,4},{5,20},{6,6},{7,22},{8,8},{9,24},{... | collective-permute-start | bytes 589832 | tf_op jit(solution)/shard_map/ppermute | solution.py:452
  241.5 5.7 %collective-permute-start.40 = (bf16[1,144,768]{2,1,0:T(8,128)(2,1)}, bf16[1,144,768]{2,1,0:T(8,128)(2,1)}, u32[]{:S(2)}, u32[]{:S(2)}) collective-permute-start(bf16[1,144,768]{2,1,0:T(8,128)(2,1)} %constant_dynamic-slice_fusion), channel_id=1, source_target_pairs={{0,2},{1,5},{2,0},{3,7},{4,6},{5,1},{6,4},{7,3},{8,10},{9,13},{10,... | collective-permute-start | bytes 663560 | tf_op jit(solution)/shard_map/ppermute | solution.py:504
  242.6 21.6 %copy-start.44 = (bf16[2,272,384]{2,1,0:T(8,128)(2,1)S(1)}, bf16[2,272,384]{2,1,0:T(8,128)(2,1)}, u32[]{:S(2)}) copy-start(bf16[2,272,384]{2,1,0:T(8,128)(2,1)} %add_convert_fusion.3) | copy-start | bytes 1253380
  242.6 25.0 %copy-start.51 = (bf16[192,512]{1,0:T(8,128)(2,1)S(1)}, bf16[192,512]{1,0:T(8,128)(2,1)}, u32[]{:S(2)}) copy-start(bf16[192,512]{1,0:T(8,128)(2,1)} %get-tuple-element.162) | copy-start | bytes 589828
  242.7 26.6 %copy-start.50 = (bf16[192,512]{1,0:T(8,128)(2,1)S(1)}, bf16[192,512]{1,0:T(8,128)(2,1)}, u32[]{:S(2)}) copy-start(bf16[192,512]{1,0:T(8,128)(2,1)} %get-tuple-element.161) | copy-start | bytes 589828
  242.7 8.6 %collective-permute-start.32 = (bf16[192,512]{1,0:T(8,128)(2,1)}, bf16[192,512]{1,0:T(8,128)(2,1)S(1)}, u32[]{:S(2)}, u32[]{:S(2)}) collective-permute-start(bf16[192,512]{1,0:T(8,128)(2,1)} %get-tuple-element.165), channel_id=1, source_target_pairs={{0,24},{1,8},{2,26},{3,10},{4,28},{5,12},{6,30},{7,14},{8,16},{9,0... | collective-permute-start | bytes 589832 | tf_op jit(solution)/shard_map/ppermute | solution.py:452
  242.7 12.9 %collective-permute-start.35 = (bf16[192,512]{1,0:T(8,128)(2,1)}, bf16[192,512]{1,0:T(8,128)(2,1)S(1)}, u32[]{:S(2)}, u32[]{:S(2)}) collective-permute-start(bf16[192,512]{1,0:T(8,128)(2,1)} %get-tuple-element.163), channel_id=1, source_target_pairs={{0,8},{1,24},{2,10},{3,26},{4,12},{5,28},{6,14},{7,30},{8,0},{9,16... | collective-permute-start | bytes 589832 | tf_op jit(solution)/shard_map/ppermute | solution.py:452
  246.7 17.5 %collective-permute-start.44 = (bf16[272,384]{1,0:T(8,128)(2,1)S(1)}, bf16[272,384]{1,0:T(8,128)(2,1)S(1)}, u32[]{:S(2)}, u32[]{:S(2)}) collective-permute-start(bf16[272,384]{1,0:T(8,128)(2,1)S(1)} %dynamic-slice_bitcast_fusion.1), channel_id=1, source_target_pairs={{0,16},{8,24},{16,0},{24,8},{1,17},{9,25},{17,1},{25,9},{2,18},{10... | collective-permute-start | bytes 626696 | tf_op jit(solution)/shard_map/ppermute | solution.py:438
  255.7 10.8 %collective-permute-start.41 = (bf16[144,192]{1,0:T(8,128)(2,1)S(1)}, bf16[144,192]{1,0:T(8,128)(2,1)S(1)}, u32[]{:S(2)}, u32[]{:S(2)}) collective-permute-start(bf16[144,192]{1,0:T(8,128)(2,1)S(1)} %get-tuple-element.183), channel_id=1, source_target_pairs={{0,16},{8,24},{16,0},{24,8},{1,17},{9,25},{17,1},{25,9},{2,18},{10... | collective-permute-start | bytes 165896 | tf_op jit(solution)/shard_map/ppermute | solution.py:438
  256.0 10.6 %collective-permute-start.42 = (bf16[144,192]{1,0:T(8,128)(2,1)S(1)}, bf16[144,192]{1,0:T(8,128)(2,1)S(1)}, u32[]{:S(2)}, u32[]{:S(2)}) collective-permute-start(bf16[144,192]{1,0:T(8,128)(2,1)S(1)} %get-tuple-element.185), channel_id=1, source_target_pairs={{0,8},{8,0},{16,24},{24,16},{1,9},{9,1},{17,25},{25,17},{2,10},{10... | collective-permute-start | bytes 165896 | tf_op jit(solution)/shard_map/ppermute | solution.py:438
  256.0 10.6 %collective-permute-start.43 = (bf16[144,192]{1,0:T(8,128)(2,1)S(1)}, bf16[144,192]{1,0:T(8,128)(2,1)S(1)}, u32[]{:S(2)}, u32[]{:S(2)}) collective-permute-start(bf16[144,192]{1,0:T(8,128)(2,1)S(1)} %get-tuple-element.184), channel_id=1, source_target_pairs={{0,24},{8,16},{16,8},{24,0},{1,25},{9,17},{17,9},{25,1},{2,26},{10... | collective-permute-start | bytes 165896 | tf_op jit(solution)/shard_map/ppermute | solution.py:438
  266.6 13.3 %copy-start.32 = (f32[512,768]{1,0:T(8,128)S(1)}, f32[512,768]{1,0:T(8,128)}, u32[]{:S(2)}) copy-start(f32[512,768]{1,0:T(8,128)} %copy-done.31) | copy-start | bytes 4718596
  266.7 13.2 %copy-start.7 = (bf16[1,512,768]{2,1,0:T(8,128)(2,1)S(1)}, bf16[1,512,768]{2,1,0:T(8,128)(2,1)}, u32[]{:S(2)}) copy-start(bf16[1,512,768]{2,1,0:T(8,128)(2,1)} %param.8) | copy-start | bytes 2359300
  266.7 13.2 %copy-start.14 = (bf16[192,512]{1,0:T(8,128)(2,1)S(1)}, bf16[192,512]{1,0:T(8,128)(2,1)}, u32[]{:S(2)}) copy-start(bf16[192,512]{1,0:T(8,128)(2,1)} %copy-done.13) | copy-start | bytes 589828
  266.7 13.2 %copy-start.16 = (bf16[192,512]{1,0:T(8,128)(2,1)S(1)}, bf16[192,512]{1,0:T(8,128)(2,1)}, u32[]{:S(2)}) copy-start(bf16[192,512]{1,0:T(8,128)(2,1)} %copy-done.15) | copy-start | bytes 589828
  266.7 13.1 %copy-start.18 = (bf16[192,512]{1,0:T(8,128)(2,1)S(1)}, bf16[192,512]{1,0:T(8,128)(2,1)}, u32[]{:S(2)}) copy-start(bf16[192,512]{1,0:T(8,128)(2,1)} %copy-done.17) | copy-start | bytes 589828
  266.7 13.1 %copy-start.20 = (bf16[192,512]{1,0:T(8,128)(2,1)S(1)}, bf16[192,512]{1,0:T(8,128)(2,1)}, u32[]{:S(2)}) copy-start(bf16[192,512]{1,0:T(8,128)(2,1)} %copy-done.19) | copy-start | bytes 589828
  266.8 13.1 %copy-start.22 = (bf16[192,512]{1,0:T(8,128)(2,1)S(1)}, bf16[192,512]{1,0:T(8,128)(2,1)}, u32[]{:S(2)}) copy-start(bf16[192,512]{1,0:T(8,128)(2,1)} %copy-done.21) | copy-start | bytes 589828
  266.8 13.1 %copy-start.24 = (bf16[192,512]{1,0:T(8,128)(2,1)S(1)}, bf16[192,512]{1,0:T(8,128)(2,1)}, u32[]{:S(2)}) copy-start(bf16[192,512]{1,0:T(8,128)(2,1)} %copy-done.23) | copy-start | bytes 589828
  266.9 6.2 %collective-permute-start.45 = (bf16[1,416,384]{2,1,0:T(8,128)(2,1)S(1)}, bf16[1,416,384]{2,1,0:T(8,128)(2,1)S(1)}, u32[]{:S(2)}, u32[]{:S(2)}) collective-permute-start(bf16[1,416,384]{2,1,0:T(8,128)(2,1)S(1)} %maximum_bitcast_fusion), channel_id=1, source_target_pairs={{0,2},{1,5},{2,0},{3,7},{4,6},{5,1},{6,4},{7,3},{8,10},{9,13},{10,... | collective-permute-start | bytes 958472 | tf_op jit(solution)/shard_map/ppermute | solution.py:504
  267.7 7.8 %collective-permute-start.36 = (bf16[192,512]{1,0:T(8,128)(2,1)S(1)}, bf16[192,512]{1,0:T(8,128)(2,1)S(1)}, u32[]{:S(2)}, u32[]{:S(2)}) collective-permute-start(bf16[192,512]{1,0:T(8,128)(2,1)S(1)} %copy-done.51), channel_id=1, source_target_pairs={{0,16},{1,0},{2,18},{3,2},{4,20},{5,4},{6,22},{7,6},{8,24},{9,8},{... | collective-permute-start | bytes 589832 | tf_op jit(solution)/shard_map/ppermute | solution.py:452
  269.2 9.7 %collective-permute-start.37 = (bf16[192,512]{1,0:T(8,128)(2,1)S(1)}, bf16[192,512]{1,0:T(8,128)(2,1)S(1)}, u32[]{:S(2)}, u32[]{:S(2)}) collective-permute-start(bf16[192,512]{1,0:T(8,128)(2,1)S(1)} %copy-done.50), channel_id=1, source_target_pairs={{0,24},{1,8},{2,26},{3,10},{4,28},{5,12},{6,30},{7,14},{8,16},{9,0... | collective-permute-start | bytes 589832 | tf_op jit(solution)/shard_map/ppermute | solution.py:452
  279.0 9.6 %collective-permute-start.46 = (bf16[2,416,384]{2,1,0:T(8,128)(2,1)S(1)}, bf16[2,416,384]{2,1,0:T(8,128)(2,1)S(1)}, u32[]{:S(2)}, u32[]{:S(2)}) collective-permute-start(bf16[2,416,384]{2,1,0:T(8,128)(2,1)S(1)} %pad_maximum_fusion.7), channel_id=1, source_target_pairs={{0,4},{1,3},{2,6},{3,1},{4,0},{5,7},{6,2},{7,5},{8,12},{9,11},{10,... | collective-permute-start | bytes 1916936 | tf_op jit(solution)/shard_map/ppermute | solution.py:504
  288.8 3.4 %collective-permute-start.47 = (bf16[4,416,384]{2,1,0:T(8,128)(2,1)S(1)}, bf16[4,416,384]{2,1,0:T(8,128)(2,1)S(1)}, u32[]{:S(2)}, u32[]{:S(2)}) collective-permute-start(bf16[4,416,384]{2,1,0:T(8,128)(2,1)S(1)} %pad_maximum_fusion.4.mine_ref), channel_id=1, source_target_pairs={{0,1},{1,0},{2,3},{3,2},{4,5},{5,4},{6,7},{7,6},{8,9},{9,8},{10,11... | collective-permute-start | bytes 3833864 | tf_op jit(solution)/shard_map/ppermute | solution.py:438
  (38 other events, 129.5 us)
